TPU v7x, 128 devices: a whole 4x4x4 slice. The times are simulated.
128 devices in a mesh: row: 8 (over x, core), col: 16 (over y, z).
Axes of the slice: x: 4, y: 4, z: 4, core: 2. Of those that a mesh axis runs over, the one named last changes fastest.
Arguments:
- front_inverse: float32 [16384, 16384], P('row', 'col'), as said below
- panel_front: float32 [4, 16384, 256], P(None, 'row'), may hold values from -0.0625 to 0.0625
- panel_cross: float32 [4, 4, 256, 256], replicated, may hold values from -0.375 to 0.375
- diag_inverse: float32 [4, 256, 256], replicated, may hold values from -6 to 6
- pattern: int32 [4, 40], replicated, may hold values from 0 to 63, as said below
Outputs:
- front_columns: float32 [4, 16384, 256], P(None, ('row', 'col'))
- panel_inverse: float32 [4, 4, 256, 256], replicated
Inputs may be any that keep to these rules, and one draw needn't show every extreme that they name: `pattern`: each row holds 40 different block numbers; block 0 and block 63 are in every row. `front_inverse`: symmetric.
All inputs are finite; a program needn't handle non-finite values.
Results may differ from a plain program's by a relative error of at most 0.0001.
Values sent between devices are 32-bit elements; how exact they have to be, the bound alone decides.
A program may use at most 128 MiB of HBM per device.

v0:
```python
import jax
import jax.numpy as jnp
from jax import lax
from jax.sharding import PartitionSpec as P


def spread(array, axis, root):
    mine = lax.axis_index(axis) == root
    return lax.psum(jnp.where(mine, array, jnp.zeros_like(array)), axis)


def product(left, right):
    return jnp.dot(left, right, precision=lax.Precision.HIGHEST, preferred_element_type=jnp.float32)


def inner(left, right):
    return jnp.einsum(
        "ri,rj->ij",
        left,
        right,
        precision=lax.Precision.HIGHEST,
        preferred_element_type=jnp.float32,
    )


def shards(front_inverse, panel_front, panel_cross, diag_inverse, pattern):
    col_count = lax.axis_size("col")
    row_index = lax.axis_index("row")
    col_index = lax.axis_index("col")
    loc_rows, loc_cols = front_inverse.shape
    panels = panel_front.shape[0]
    block_width = panel_front.shape[2]
    spread_ratio = loc_rows // loc_cols
    own_count = loc_rows // col_count
    global_rows = row_index * loc_rows + jnp.arange(loc_rows, dtype=jnp.int32)
    block_ids = global_rows // block_width
    member = jnp.any(block_ids[None, :, None] == pattern[:, None, :], axis=2).astype(jnp.float32)
    masked = panel_front * member[:, :, None]
    own_first = col_index * own_count
    own_member = lax.dynamic_slice_in_dim(member, own_first, own_count, 1)
    own_panel = lax.dynamic_slice_in_dim(masked, own_first, own_count, 1)
    columns = [None] * panels
    inverse_table = {}
    for k in reversed(range(panels)):
        later_panels = list(range(k + 1, panels))
        segment = lax.dynamic_slice_in_dim(
            masked[k], col_index % spread_ratio * loc_cols, loc_cols, 0
        )
        columns_here = spread(segment, "row", col_index // spread_ratio)
        direct = lax.psum_scatter(
            product(front_inverse, columns_here), "col", scatter_dimension=0, tiled=True
        )
        for j in later_panels:
            direct = direct + product(columns[j], panel_cross[j, k])
        columns[k] = -own_member[k][:, None] * direct
        local_list = [inner(own_panel[k], columns[k])] + [
            inner(columns[j], own_panel[k]) for j in later_panels
        ]
        summed = lax.psum(jnp.stack(local_list), ("row", "col"))
        diag_block = diag_inverse[k] - summed[0]
        for place, j in enumerate(later_panels):
            running = summed[1 + place]
            for i in later_panels:
                running = running + product(inverse_table[j, i], panel_cross[i, k])
            cross_inv = -running
            inverse_table[j, k] = cross_inv
            inverse_table[k, j] = cross_inv.T
            diag_block = diag_block - inner(panel_cross[j, k], cross_inv)
        inverse_table[k, k] = diag_block
    panel_inverse = jnp.stack(
        [jnp.stack([inverse_table[j, k] for k in range(panels)]) for j in range(panels)]
    )
    return (jnp.stack(columns), panel_inverse)


def solution(mesh):
    in_specs = (P("row", "col"), P(None, "row", None), P(), P(), P())
    out_specs = (P(None, ("row", "col"), None), P())
    return jax.shard_map(shards, mesh=mesh, in_specs=in_specs, out_specs=out_specs, check_vma=False)
```

profile of v0, /device:TPU:1, one launch (start us, length us, event | category | flops | bytes accessed | tf_op | source)
XLA Modules:
  0.0 640.8 jit_solution(13517373745266338267)
XLA Ops:
  7.3 0.9 compare_reduce_fusion
  8.2 4.1 broadcast_multiply_fusion
  12.4 3.2 copy-done
  15.6 2.9 fusion.101
  18.4 3.1 select_bitcast_fusion.2
  21.6 1.5 select_bitcast_fusion
  23.1 74.3 %all-reduce.7.cloned.1.call-done = (f32[1024,256]{1,0:T(8,128)}, f32[1024,256]{1,0:T(8,128)}, f32[1024,256]{1,0:T(8,128)}, f32[1024,256]{1,0:T(8,128)}) async-done(((f32[1024,256]{1,0:T(8,128)}, f32[1024,256]{1,0:T(8,128)}, f32[1024,256]{1,0:T(8,128)}, f32[1024,256]{1,0:T(8,128)}), (f32[1024,256]{1,0:T(8,128)}, f32[1024,256]{1,0:T(8,128)}, f32[1024,256]{1,0:T(8,128)}, ...) | async-done | bytes 4194320 | tf_op jit(solution)/shard_map/psum | solution.py:9
  97.4 17.2 %convolution_bitcast_fusion = f32[2048,256]{0,1:T(8,128)} fusion(f32[1024,256]{1,0:T(8,128)} %get-tuple-element.10, f32[2048,1024]{1,0:T(8,128)} %param.5), kind=kOutput, calls=%fused_computation.2 | convolution fusion | flops 6442450944 | bytes 11534336 | tf_op jit(solution)/shard_map/dot_general | solution.py:13
  115.2 16.9 %convolution_bitcast_fusion.1 = f32[2048,256]{0,1:T(8,128)} fusion(f32[1024,256]{1,0:T(8,128)S(1)} %copy-done.12, f32[2048,1024]{1,0:T(8,128)} %param.5), kind=kOutput, calls=%fused_computation.3 | convolution fusion | flops 6442450944 | bytes 11534336 | tf_op jit(solution)/shard_map/dot_general | solution.py:13
  132.4 16.9 %convolution_bitcast_fusion.2 = f32[2048,256]{0,1:T(8,128)} fusion(f32[1024,256]{1,0:T(8,128)S(1)} %copy-done.11, f32[2048,1024]{1,0:T(8,128)} %param.5), kind=kOutput, calls=%fused_computation.4 | convolution fusion | flops 6442450944 | bytes 11534336 | tf_op jit(solution)/shard_map/dot_general | solution.py:13
  149.7 16.9 %convolution_bitcast_fusion.3 = f32[2048,256]{0,1:T(8,128)} fusion(f32[1024,256]{1,0:T(8,128)S(1)} %copy-done.10, f32[2048,1024]{1,0:T(8,128)} %param.5), kind=kOutput, calls=%fused_computation.5 | convolution fusion | flops 6442450944 | bytes 11534336 | tf_op jit(solution)/shard_map/dot_general | solution.py:13
  166.9 22.6 %reduce-scatter.11.cloned.1.call-done = f32[128,256]{0,1:T(8,128)} async-done(((f32[2048,256]{0,1:T(8,128)}), f32[128,256]{0,1:T(8,128)}) %reduce-scatter.11.cloned.1.call-update) | async-done | bytes 131088 | tf_op jit(solution)/shard_map/reduce_scatter | solution.py:50
  189.5 77.2 %reduce-scatter.9.cloned.1.call-done = f32[128,256]{0,1:T(8,128)} async-done(((f32[2048,256]{0,1:T(8,128)}), f32[128,256]{0,1:T(8,128)}) %reduce-scatter.9.cloned.1.call-update) | async-done | bytes 131088 | tf_op jit(solution)/shard_map/reduce_scatter | solution.py:50
  266.8 1.6 fusion.15
  268.4 1.3 convolution_bitcast_fusion.17
  269.7 1.3 convolution_bitcast_fusion.14
  271.0 72.6 %reduce-scatter.7.cloned.1.call-done = f32[128,256]{0,1:T(8,128)} async-done(((f32[2048,256]{0,1:T(8,128)}), f32[128,256]{0,1:T(8,128)}) %reduce-scatter.7.cloned.1.call-update) | async-done | bytes 131088 | tf_op jit(solution)/shard_map/reduce_scatter | solution.py:50
  343.6 1.6 convolution_add_fusion.18
  345.1 1.6 fusion.14
  346.8 1.3 convolution_bitcast_fusion.15
  348.1 1.3 convolution_bitcast_fusion.18
  349.4 1.3 convolution_bitcast_fusion.12
  350.7 69.9 %reduce-scatter.5.cloned.1.call-done = f32[128,256]{0,1:T(8,128)} async-done(((f32[2048,256]{0,1:T(8,128)}), f32[128,256]{0,1:T(8,128)}) %reduce-scatter.5.cloned.1.call-update) | async-done | bytes 131088 | tf_op jit(solution)/shard_map/reduce_scatter | solution.py:50
  420.5 1.6 convolution_add_fusion.16
  422.1 1.5 convolution_add_fusion.15
  423.7 1.5 fusion.13
  425.2 1.3 convolution_bitcast_fusion.19
  426.5 1.3 convolution_bitcast_fusion.11
  428.7 1.3 convolution_bitcast_fusion.13
  430.0 1.0 pad_maximum_fusion.2
  431.0 1.4 convolution_bitcast_fusion.16
  432.3 1.0 pad_maximum_fusion.1
  433.4 2.0 convolution_bitcast_fusion.10
  435.5 1.0 copy.66
  436.5 152.4 %all-reduce.5.cloned.1.call-done = (f32[1,256,256]{2,1,0:T(8,128)}, f32[2,256,256]{1,2,0:T(8,128)}, f32[3,256,256]{2,1,0:T(8,128)}, f32[4,256,256]{2,1,0:T(8,128)}) async-done(((f32[1,256,256]{2,1,0:T(8,128)}, f32[2,256,256]{1,2,0:T(8,128)}, f32[3,256,256]{2,1,0:T(8,128)}, f32[4,256,256]{2,1,0:T(8,128)}), (f32[1,256,256]{2,1,0:T(8,128)}, f32[2,256,256]{1,2,0:T(8,128)}, f32[3,256,256]{2,1,0:T(8,128)}, ...) | async-done | bytes 2621456 | tf_op jit(solution)/shard_map/psum | solution.py:59
  588.9 1.0 fusion.103
  590.1 1.6 fusion.12
  591.7 1.5 fusion.11
  593.2 0.8 copy.64
  594.1 2.3 convolution_add_fusion.10
  596.4 1.6 convolution_add_fusion.12
  598.9 1.3 fusion.10
  600.2 1.6 fusion.9
  601.8 1.4 fusion.8
  603.3 1.3 convolution_add_fusion.2
  604.7 1.8 fusion.7
  606.5 0.8 copy.61
  607.3 1.5 convolution_add_fusion.1
  608.9 1.3 fusion.2
  610.2 0.9 copy.60
  611.2 1.5 convolution_add_fusion.8
  612.8 1.5 convolution_add_fusion.7
  614.3 1.6 fusion.6
  615.9 1.7 fusion.5
  617.7 1.5 convolution_add_fusion.5
  619.3 1.5 convolution_add_fusion.4
  620.9 1.6 fusion.4
  622.5 1.5 fusion.3
  624.0 2.3 fusion.1
  626.3 0.8 copy.62
  627.2 1.0 maximum_bitcast_fusion.1
  628.2 1.3 copy.65
  629.6 1.1 maximum_bitcast_fusion.2
  631.0 2.4 pad_maximum_fusion
  (51 shorter events, 4.0 us)
Async XLA Ops:
  7.2 90.3 %all-reduce.7.cloned.1.call-start = ((), (), s32[]{:S(2)}) async-start(), calls=%async_computation.9 | async-start | bytes 8388608 | tf_op jit(solution)/shard_map/psum | solution.py:9
  12.3 3.2 copy-start
  18.4 3.1 copy-start.2
  23.1 166.5 %reduce-scatter.11.cloned.1.call-start = ((), (), s32[]{:S(2)}) async-start(), calls=%async_computation.7 | async-start | bytes 2228224 | tf_op jit(solution)/shard_map/reduce_scatter | solution.py:50
  97.4 17.8 %copy-start.12 = (f32[1024,256]{1,0:T(8,128)S(1)}, f32[1024,256]{1,0:T(8,128)}, u32[]{:S(2)}) copy-start(f32[1024,256]{1,0:T(8,128)} %get-tuple-element.11) | copy-start | bytes 3145732
  114.6 152.2 %reduce-scatter.9.cloned.1.call-start = ((), (), s32[]{:S(2)}) async-start(), calls=%async_computation.6 | async-start | bytes 2228224 | tf_op jit(solution)/shard_map/reduce_scatter | solution.py:50
  115.2 17.2 %copy-start.11 = (f32[1024,256]{1,0:T(8,128)S(1)}, f32[1024,256]{1,0:T(8,128)}, u32[]{:S(2)}) copy-start(f32[1024,256]{1,0:T(8,128)} %get-tuple-element.12) | copy-start | bytes 3145732
  132.2 211.4 %reduce-scatter.7.cloned.1.call-start = ((), (), s32[]{:S(2)}) async-start(), calls=%async_computation.5 | async-start | bytes 2228224 | tf_op jit(solution)/shard_map/reduce_scatter | solution.py:50
  132.4 17.2 %copy-start.10 = (f32[1024,256]{1,0:T(8,128)S(1)}, f32[1024,256]{1,0:T(8,128)}, u32[]{:S(2)}) copy-start(f32[1024,256]{1,0:T(8,128)} %get-tuple-element.13) | copy-start | bytes 3145732
  149.4 271.1 %reduce-scatter.5.cloned.1.call-start = ((), (), s32[]{:S(2)}) async-start(), calls=%async_computation.4 | async-start | bytes 2228224 | tf_op jit(solution)/shard_map/reduce_scatter | solution.py:50
  166.6 422.3 %all-reduce.5.cloned.1.call-start = ((), (), s32[]{:S(2)}) async-start(), calls=%async_computation.8 | async-start | bytes 5242880 | tf_op jit(solution)/shard_map/psum | solution.py:59
  189.5 234.1 %copy-start.1 = (f32[128,256]{0,1:T(8,128)S(1)}, f32[128,256]{0,1:T(8,128)}, u32[]{:S(2)}) copy-start(f32[128,256]{0,1:T(8,128)} %reduce-scatter.11.cloned.1.call-done) | copy-start | bytes 393220
  431.0 158.0 %copy-start.4 = (f32[4,256,256]{2,1,0:T(8,128)S(1)}, f32[4,256,256]{2,1,0:T(8,128)}, u32[]{:S(2)}) copy-start(f32[4,256,256]{2,1,0:T(8,128)} %param.8) | copy-start | bytes 3145732
  591.7 11.5 %copy-start.5 = (f32[4,256,256]{2,1,0:T(8,128)S(1)}, f32[4,256,256]{2,1,0:T(8,128)}, u32[]{:S(2)}) copy-start(f32[4,256,256]{2,1,0:T(8,128)} %get-tuple-element.9) | copy-start | bytes 3145732
  620.9 8.7 %copy-start.7 = (f32[1,256,256]{2,1,0:T(8,128)S(1)}, f32[1,256,256]{2,1,0:T(8,128)}, u32[]{:S(2)}) copy-start(f32[1,256,256]{2,1,0:T(8,128)} %copy.64) | copy-start | bytes 786436
  624.0 5.6 copy-start.6
  629.5 1.3 copy-start.8
  629.5 1.3 copy-start.9
  629.5 1.5 copy-start.3
Sparse Core Ops, SparseCore 0:
  23.2 74.1 all-reduce.6
  114.7 74.7 reduce-scatter.10
  193.2 73.5 reduce-scatter.8
  269.9 73.6 reduce-scatter.6
  347.0 73.4 reduce-scatter.4
  435.6 153.3 all-reduce.4
where the time goes:
time: 648 us; the launch traced here: 641 us
  waiting for transfers between devices  469 us (72%)
  matrix products  124 us (19%)
  other arithmetic  18.4 us (3%)
  between operations  15.1 us (2%)
  local copies, waits for them, and re-layouts  13.2 us (2%)
    reduce_scatter x4, waiting for transfers between devices, shards(): lax.psum_scatter(product(front_inverse, columns_here), 'col', scatter_dim...  242 us
    psum x1, waiting for transfers between devices, shards(): summed = lax.psum(jnp.stack(local_list), ('row', 'col'))  152 us
    dot_general x24, matrix products, product(): jnp.dot(left, right, precision=lax.Precision.HIGHEST, preferred_element_t...  99.3 us
    psum x1, waiting for transfers between devices, spread(): return lax.psum(jnp.where(mine, array, jnp.zeros_like(array)), axis)  74.3 us
    dot_general x16, matrix products, inner(): jnp.einsum('ri,rj->ij', left, right, precision=lax.Precision.HIGHEST, pre...  24.2 us
  transfers between devices with their start and end apart: 6, of which 6 were waited for; matrix products, arithmetic and copies ran while one was open for 10% of the time, Pallas kernels for 0%

commit v1 on v0

v1 whole, which is shorter than its diff:
```python
import jax
import jax.numpy as jnp
from jax import lax
from jax.sharding import PartitionSpec as P

HIGH = lax.Precision.HIGH


def product(left, right):
    return jnp.dot(left, right, precision=HIGH, preferred_element_type=jnp.float32)


def inner(left, right):
    return jnp.einsum(
        "ri,rj->ij", left, right, precision=HIGH, preferred_element_type=jnp.float32
    )


def shards(front_inverse, panel_front, panel_cross, diag_inverse, pattern):
    rows, cols = lax.axis_size("row"), lax.axis_size("col")
    row_index, col_index = lax.axis_index("row"), lax.axis_index("col")
    loc_rows, loc_cols = front_inverse.shape
    panels, _, width = panel_front.shape
    own = loc_cols // rows
    ids = (row_index * loc_rows + jnp.arange(loc_rows, dtype=jnp.int32)) // width
    member = jnp.any(ids[None, :, None] == pattern[:, None, :], axis=2).astype(jnp.float32)
    masked = panel_front * member[:, :, None]
    partial = jnp.einsum(
        "rc,krb->kcb", front_inverse, masked, precision=HIGH, preferred_element_type=jnp.float32
    )
    direct = lax.psum_scatter(partial, "row", scatter_dimension=1, tiled=True)
    placed = [(i, i % rows * cols + i // rows) for i in range(rows * cols)]
    own_panel = lax.dynamic_slice_in_dim(masked, col_index * own, own, 1)
    own_panel = lax.ppermute(own_panel, ("row", "col"), placed)
    block = (col_index * loc_cols + row_index * own) // width
    own_member = jnp.any(pattern == block, axis=1).astype(jnp.float32)
    columns = [None] * panels
    table = {}
    for k in reversed(range(panels)):
        value = direct[k]
        for j in range(k + 1, panels):
            value = value + product(columns[j], panel_cross[j, k])
        columns[k] = -own_member[k] * value
    pairs = [(j, k) for k in range(panels) for j in range(k, panels)]
    grams = lax.psum(jnp.stack([inner(columns[j], own_panel[k]) for j, k in pairs]), ("row", "col"))
    grams = {pair: grams[i] for i, pair in enumerate(pairs)}
    for k in reversed(range(panels)):
        later = range(k + 1, panels)
        diag_block = diag_inverse[k] - grams[k, k].T
        for j in later:
            running = grams[j, k]
            for i in later:
                running = running + product(table[j, i], panel_cross[i, k])
            table[j, k] = -running
            table[k, j] = -running.T
            diag_block = diag_block + inner(panel_cross[j, k], running)
        table[k, k] = diag_block
    panel_inverse = jnp.stack(
        [jnp.stack([table[j, k] for k in range(panels)]) for j in range(panels)]
    )
    back = [(b, a) for a, b in placed]
    return lax.ppermute(jnp.stack(columns), ("row", "col"), back), panel_inverse


def solution(mesh):
    in_specs = (P("row", "col"), P(None, "row", None), P(), P(), P())
    out_specs = (P(None, ("row", "col"), None), P())
    return jax.shard_map(shards, mesh=mesh, in_specs=in_specs, out_specs=out_specs, check_vma=False)
```

time: 648 us -> 313 us (0.48)
  waiting for transfers between devices: 469 us -> 197 us
  matrix products: 124 us -> 52.5 us
  starting transfers between devices: 1.41 us -> 11.6 us
    reduce_scatter x4 -> x1, waiting for transfers between devices: 242 us -> 45.1 us  [shards(): direct = lax.psum_scatter(partial, 'row', scatter_dimension=1, tiled=True)]
    psum x2 -> x1, waiting for transfers between devices: 227 us -> 140 us  [shards(): lax.psum(jnp.stack([inner(columns[j], own_panel[k]) for j, k in pairs]),...]
    dot_general x40 -> x37, matrix products: 124 us -> 52.5 us  [the longest x20 26.5 us: product(): jnp.dot(left, right, precision=HIGH, preferred_element_type=jnp.float32)]
    ppermute x0 -> x2, waiting for transfers between devices: none -> 12.5 us  [the longest x1 12.5 us: shards(): lax.ppermute(jnp.stack(columns), ('row', 'col'), back)]
    ppermute x0 -> x2, starting transfers between devices: none -> 11.5 us  [the longest x1 7.08 us: shards(): own_panel = lax.ppermute(own_panel, ('row', 'col'), placed)]
  transfers between devices with their start and end apart: 6 -> 4, of which waited for: 6 -> 3; matrix products, arithmetic and copies ran while one was open for 10% -> 5% of each run, Pallas kernels for 0% -> 0%
where the time goes in v1:
time: 313 us; the launch traced here: 312 us
  waiting for transfers between devices  197 us (63%)
  matrix products  52.5 us (17%)
  between operations  17.1 us (5%)
  other arithmetic  16.7 us (5%)
  local copies, waits for them, and re-layouts  16.6 us (5%)
  starting transfers between devices  11.6 us (4%)
    psum x1, waiting for transfers between devices, shards(): lax.psum(jnp.stack([inner(columns[j], own_panel[k]) for j, k in pairs]),...  140 us
    reduce_scatter x1, waiting for transfers between devices, shards(): direct = lax.psum_scatter(partial, 'row', scatter_dimension=1, tiled=True)  45.1 us
    dot_general x20, matrix products, product(): jnp.dot(left, right, precision=HIGH, preferred_element_type=jnp.float32)  26.5 us
    dot_general x1, matrix products, shards(): jnp.einsum('rc,krb->kcb', front_inverse, masked, precision=HIGH, preferre...  15.1 us
    ppermute x1, waiting for transfers between devices, shards(): lax.ppermute(jnp.stack(columns), ('row', 'col'), back)  12.5 us
    dot_general x16, matrix products, inner(): jnp.einsum('ri,rj->ij', left, right, precision=HIGH, preferred_element_ty...  10.8 us
    unnamed x30, local copies, waits for them, and re-layouts  7.83 us
    ppermute x1, starting transfers between devices, shards(): own_panel = lax.ppermute(own_panel, ('row', 'col'), placed)  7.08 us
  transfers between devices with their start and end apart: 4, of which 3 were waited for; matrix products, arithmetic and copies ran while one was open for 5% of the time, Pallas kernels for 0%

profile of v1, /device:TPU:1, one launch (start us, length us, event | category | flops | bytes accessed | tf_op | source)
XLA Modules:
  0.0 311.8 jit_solution(3276272958958532953)
XLA Ops:
  7.2 0.9 compare_reduce_fusion
  8.2 4.2 %broadcast_multiply_fusion = f32[4,2048,256]{2,1,0:T(8,128)S(1)} fusion(f32[4,2048,256]{2,1,0:T(8,128)} %param.6, f32[4,2048]{1,0:T(4,128)S(1)} %convert_element_type.11), kind=kLoop, calls=%fused_computation.3 | loop fusion | flops 2097152 | bytes 16809984 | tf_op jit(solution)/shard_map/mul | solution.py:27
  12.5 3.5 %copy-done = f32[4,2048,256]{2,1,0:T(8,128)} copy-done((f32[4,2048,256]{2,1,0:T(8,128)}, f32[4,2048,256]{2,1,0:T(8,128)S(1)}, u32[]{:S(2)}) %copy-start) | copy-done | bytes 8388632
  15.9 15.1 %fusion.2 = f32[4,1024,256]{1,2,0:T(8,128)} fusion(f32[4,2048,256]{2,1,0:T(8,128)S(1)} %broadcast_multiply_fusion, f32[2048,1024]{1,0:T(8,128)S(1)} %copy-done.10), kind=kOutput, calls=%fused_computation.4 | convolution fusion | flops 12884901888 | bytes 20971520 | tf_op jit(solution)/shard_map/rc,krb->kcb/dot_general | solution.py:28
  31.2 1.1 constant_dynamic-slice_fusion
  32.2 7.1 %collective-permute-start.1 = (f32[4,128,256]{2,1,0:T(8,128)S(1)}, f32[4,128,256]{2,1,0:T(8,128)S(1)}, u32[]{:S(2)}, u32[]{:S(2)}) collective-permute-start(f32[4,128,256]{2,1,0:T(8,128)S(1)} %constant_dynamic-slice_fusion), channel_id=1, source_target_pairs={{0,0},{1,16},{2,32},{3,48},{4,64},{5,80},{6,96},{7,112},{8,1},{9,1... | collective-permute-start | bytes 1572872 | tf_op jit(solution)/shard_map/ppermute | solution.py:34
  39.5 0.7 fusion.98
  42.6 45.1 %reduce-scatter.2.cloned.1.call-done = f32[4,128,256]{1,2,0:T(8,128)} async-done(((f32[4,1024,256]{1,2,0:T(8,128)}), f32[4,128,256]{1,2,0:T(8,128)}) %reduce-scatter.2.cloned.1.call-update) | async-done | bytes 524304 | tf_op jit(solution)/shard_map/reduce_scatter | solution.py:31
  87.7 0.9 slice_multiply_fusion
  88.6 1.4 fusion.24
  90.0 1.4 convolution_add_fusion.18
  91.3 1.3 fusion.23
  92.7 1.4 convolution_add_fusion.16
  94.1 1.3 convolution_add_fusion.15
  95.4 1.3 fusion.22
  96.8 0.3 fusion.21
  97.6 0.3 fusion.18
  97.8 0.3 fusion.17
  98.1 0.3 fusion.16
  98.3 0.3 fusion.15
  98.6 0.3 fusion.14
  98.9 0.3 fusion.13
  99.1 0.3 fusion.12
  99.4 1.5 copy-done.1
  100.9 1.0 pad_maximum_fusion.1
  102.0 4.5 %collective-permute-start = (f32[4,128,256]{1,2,0:T(8,128)S(1)}, f32[4,128,256]{1,2,0:T(8,128)S(1)}, u32[]{:S(2)}, u32[]{:S(2)}) collective-permute-start(f32[4,128,256]{1,2,0:T(8,128)S(1)} %pad_maximum_fusion.1), channel_id=1, source_target_pairs={{0,0},{16,1},{32,2},{48,3},{64,4},{80,5},{96,6},{112,7},{1,8},{17,... | collective-permute-start | bytes 1572872 | tf_op jit(solution)/shard_map/ppermute | solution.py:62
  106.4 1.0 slice.143
  107.5 12.5 %collective-permute-done = f32[4,128,256]{1,2,0:T(8,128)S(1)} collective-permute-done((f32[4,128,256]{1,2,0:T(8,128)S(1)}, f32[4,128,256]{1,2,0:T(8,128)S(1)}, u32[]{:S(2)}, u32[]{:S(2)}) %collective-permute-start) | collective-permute-done | bytes 524320 | tf_op jit(solution)/shard_map/ppermute | solution.py:62
  120.0 1.0 copy.66
  121.0 139.8 %all-reduce.2.cloned.1.call-done = f32[10,256,256]{2,1,0:T(8,128)} async-done(((f32[10,256,256]{2,1,0:T(8,128)}), f32[10,256,256]{2,1,0:T(8,128)}) %all-reduce.2.cloned.1.call-update) | async-done | bytes 2621456 | tf_op jit(solution)/shard_map/psum | solution.py:45
  260.8 2.1 fusion.96
  263.3 1.3 convolution_add_fusion.13
  264.6 0.7 negate_bitcast_fusion.9
  265.4 0.9 copy.64
  266.2 1.4 convolution_add_fusion.10
  267.7 1.2 convolution_add_fusion.9
  269.0 1.3 fusion.11
  270.4 1.3 convolution_add_fusion.12
  271.7 1.2 convolution_add_fusion.11
  272.9 1.0 negate_bitcast_fusion.5
  274.0 1.3 convolution_add_fusion.2
  275.3 1.3 convolution_add_fusion.1
  276.6 1.2 convolution_add_fusion
  277.9 0.8 fusion.97
  278.8 1.3 convolution_add_fusion.5
  280.2 1.3 convolution_add_fusion.4
  281.5 1.3 convolution_add_fusion.3
  282.8 1.4 fusion.10
  284.3 1.3 fusion.9
  285.8 1.3 convolution_add_fusion.8
  287.1 1.3 convolution_add_fusion.7
  288.4 1.3 convolution_add_fusion.6
  289.8 0.9 negate_bitcast_fusion.1
  290.7 0.8 copy.63
  291.5 1.1 maximum_bitcast_fusion.1
  292.6 0.3 copy.65
  293.0 1.9 copy.62
  294.8 1.1 copy.85
  296.0 1.5 fusion.8
  297.4 1.3 fusion.7
  298.8 1.3 fusion.6
  300.1 1.1 maximum_bitcast_fusion.3
  301.4 1.1 maximum_bitcast_fusion
  302.5 2.4 pad_maximum_fusion
  (39 shorter events, 1.7 us)
Async XLA Ops:
  7.2 80.5 %reduce-scatter.2.cloned.1.call-start = ((), (), s32[]{:S(2)}) async-start(), calls=%async_computation.1 | async-start | bytes 4718592 | tf_op jit(solution)/shard_map/reduce_scatter | solution.py:31
  8.2 7.7 %copy-start.10 = (f32[2048,1024]{1,0:T(8,128)S(1)}, f32[2048,1024]{1,0:T(8,128)}, u32[]{:S(2)}) copy-start(f32[2048,1024]{1,0:T(8,128)} %param.5) | copy-start | bytes 25165828
  12.5 3.5 %copy-start = (f32[4,2048,256]{2,1,0:T(8,128)}, f32[4,2048,256]{2,1,0:T(8,128)S(1)}, u32[]{:S(2)}) copy-start(f32[4,2048,256]{2,1,0:T(8,128)S(1)} %broadcast_multiply_fusion) | copy-start | bytes 25165828
  31.1 8.3 %copy-start.9 = (s32[4,40]{1,0:T(4,128)S(1)}, s32[4,40]{1,0:T(4,128)}, u32[]{:S(2)}) copy-start(s32[4,40]{1,0:T(4,128)} %param.9) | copy-start | bytes 1924
  31.1 229.7 %all-reduce.2.cloned.1.call-start = ((), (), s32[]{:S(2)}) async-start(), calls=%async_computation.2 | async-start | bytes 5242880 | tf_op jit(solution)/shard_map/psum | solution.py:45
  32.2 64.5 %collective-permute-start.1 = (f32[4,128,256]{2,1,0:T(8,128)S(1)}, f32[4,128,256]{2,1,0:T(8,128)S(1)}, u32[]{:S(2)}, u32[]{:S(2)}) collective-permute-start(f32[4,128,256]{2,1,0:T(8,128)S(1)} %constant_dynamic-slice_fusion), channel_id=1, source_target_pairs={{0,0},{1,16},{2,32},{3,48},{4,64},{5,80},{6,96},{7,112},{8,1},{9,1... | collective-permute-start | bytes 1572872 | tf_op jit(solution)/shard_map/ppermute | solution.py:34
  96.8 2.4 copy-start.2
  99.4 1.5 copy-start.1
  100.9 162.2 %copy-start.3 = (f32[4,256,256]{2,1,0:T(8,128)S(1)}, f32[4,256,256]{2,1,0:T(8,128)}, u32[]{:S(2)}) copy-start(f32[4,256,256]{2,1,0:T(8,128)} %param.8) | copy-start | bytes 3145732
  102.0 18.1 %collective-permute-start = (f32[4,128,256]{1,2,0:T(8,128)S(1)}, f32[4,128,256]{1,2,0:T(8,128)S(1)}, u32[]{:S(2)}, u32[]{:S(2)}) collective-permute-start(f32[4,128,256]{1,2,0:T(8,128)S(1)} %pad_maximum_fusion.1), channel_id=1, source_target_pairs={{0,0},{16,1},{32,2},{48,3},{64,4},{80,5},{96,6},{112,7},{1,8},{17,... | collective-permute-start | bytes 1572872 | tf_op jit(solution)/shard_map/ppermute | solution.py:62
  293.0 7.2 %copy-start.5 = (f32[1,256,256]{2,1,0:T(8,128)S(1)}, f32[1,256,256]{2,1,0:T(8,128)}, u32[]{:S(2)}) copy-start(f32[1,256,256]{2,1,0:T(8,128)} %get-tuple-element.17) | copy-start | bytes 786436
  293.0 8.3 %copy-start.4 = (f32[1,256,256]{2,1,0:T(8,128)S(1)}, f32[1,256,256]{2,1,0:T(8,128)}, u32[]{:S(2)}) copy-start(f32[1,256,256]{2,1,0:T(8,128)} %get-tuple-element.22) | copy-start | bytes 786436
  295.9 5.4 %copy-start.6 = (f32[1,256,256]{2,1,0:T(8,128)S(1)}, f32[1,256,256]{2,1,0:T(8,128)}, u32[]{:S(2)}) copy-start(f32[1,256,256]{2,1,0:T(8,128)} %copy.63) | copy-start | bytes 786436
  295.9 5.4 %copy-start.8 = (f32[1,256,256]{2,1,0:T(8,128)S(1)}, f32[1,256,256]{2,1,0:T(8,128)}, u32[]{:S(2)}) copy-start(f32[1,256,256]{2,1,0:T(8,128)} %get-tuple-element.28) | copy-start | bytes 786436
  295.9 5.5 %copy-start.7 = (f32[256,256]{0,1:T(8,128)S(1)}, f32[256,256]{0,1:T(8,128)}, u32[]{:S(2)}) copy-start(f32[256,256]{0,1:T(8,128)} %copy.62) | copy-start | bytes 786436
Sparse Core Ops, SparseCore 0:
  31.2 56.4 reduce-scatter.1
  101.0 159.7 all-reduce.1

commit v2 on v1

v2 whole, which is shorter than its diff:
```python
import jax
import jax.numpy as jnp
from jax import lax
from jax.experimental import pallas as pl
from jax.experimental.pallas import tpu as pltpu
from jax.sharding import PartitionSpec as P

MESH = pl.DeviceIdType.MESH
F32, BF16 = jnp.float32, jnp.bfloat16
W = 256
PANELS = 4
PAIRS = [(j, k) for k in range(PANELS) for j in range(k + 1, PANELS)]
AT = {pair: i for i, pair in enumerate(PAIRS)}


def split(value):
    high = value.astype(BF16)
    return high, (value - high.astype(F32)).astype(BF16)


def dot(left, right):
    return jnp.dot(left, right, preferred_element_type=F32)


def dot3(left, right):
    return dot(left[0], right[0]) + dot(left[1], right[0]) + dot(left[0], right[1])


class Scratch:
    def __init__(self):
        self.names, self.shapes = [], []

    def add(self, name, shape, dtype=F32):
        self.names.append(name)
        self.shapes.append(pltpu.VMEM(shape, dtype))


def scratch():
    s = Scratch()
    s.add("m32", (PANELS, 2048, W))
    s.add("f32", (4, 2048, W))
    s.add("fh", (4, 2048, W), BF16)
    s.add("fl", (4, 2048, W), BF16)
    s.add("mh", (2, W, 2048), BF16)
    s.add("ml", (2, W, 2048), BF16)
    s.add("part", (PANELS, 4, 2, W, 128))
    s.add("sib", (PANELS, 4, W, 128))
    s.add("chip", (PANELS, 4, W, 128))
    s.add("r1", (PANELS, 2, 128, 128))
    s.add("r2", (PANELS, 2, W, 128))
    s.add("cols", (PANELS, 128, W))
    s.add("ch", (PANELS, 128, W), BF16)
    s.add("cl", (PANELS, 128, W), BF16)
    s.add("placed", (PANELS, 128, W))
    s.add("oh", (PANELS, W, 128), BF16)
    s.add("ol", (PANELS, W, 128), BF16)
    s.add("x32", (len(PAIRS), W, W))
    for name in ("xh", "xl", "xth", "xtl"):
        s.add(name, (len(PAIRS), W, W), BF16)
    s.add("diag", (PANELS, W, W))
    for p in range(PANELS):
        n = p + 1
        s.add(f"g{p}", (2, 4, 4, n, 8, W))
        s.add(f"gs{p}", (4, 4, n, 8, W))
        s.add(f"ga{p}", (3, 4, n, 8, W))
        s.add(f"gb{p}", (3, n, 8, W))
        s.add(f"gx{p}", (4, n, 8, W))
        s.add(f"res{p}", (2, 4, 4, n, 8, W))
    s.add("inv", (PANELS, PANELS, W, W))
    s.add("invt", (PANELS, W, W))
    s.add("pre", (W, W))
    return s


REMOTE = 128
LOCAL = 64


def kernel(names, f_hbm, m_hbm, x_hbm, diag_hbm, pat_ref, cols_hbm, inv_hbm, *refs):
    v = dict(zip(names, refs))
    send_sem, recv_sem, local_sem = refs[len(names):]
    row, col = lax.axis_index("row"), lax.axis_index("col")
    x, core = row // 2, row % 2
    y, z = col // 4, col % 4

    def at(x, y, z, core):
        return ((x % 4) * 2 + core, (y % 4) * 4 + z % 4)

    sibling = at(x, y, z, 1 - core)
    x_peer = [at(x + s, y, z, core) for s in range(4)]
    a_me, b_me = y + (z - y) * core, z + (y - z) * core
    a_peer = [at(x, y + s * (1 - core), z + s * core, core) for s in range(4)]
    b_peer = [at(x, y + s * core, z + s * (1 - core), core) for s in range(4)]
    to = col * 8 + row
    place = (to // 16, to % 16)
    here = row * 16 + col
    source = (here % 8, here // 8)
    stays = to == here

    counts = {"remote": 0, "local": 0}
    pending = []

    def remote(src, dst, device):
        i = counts["remote"]
        counts["remote"] += 1
        return pltpu.make_async_remote_copy(
            src, dst, send_sem.at[i], recv_sem.at[i], device_id=device, device_id_type=MESH
        )

    def local(src, dst):
        i = counts["local"]
        counts["local"] += 1
        return pltpu.make_async_copy(src, dst, local_sem.at[i])

    def send(src, dst, device):
        copy = remote(src, dst, device)
        copy.start()
        pending.append(copy.wait_send)
        return copy

    xs = [x + 2, x + 1, x + 3, x]
    m_copy = [local(m_hbm.at[p], v["m32"].at[p]) for p in range(PANELS)]
    f_copy = []
    for t in range(4):
        first = pl.multiple_of((xs[t] % 4) * W, W)
        f_copy.append(local(f_hbm.at[:, pl.ds(first, W)], v["f32"].at[t]))
    x_copy = [local(x_hbm.at[j, k], v["x32"].at[AT[j, k]]) for j, k in PAIRS]
    diag_copy = local(diag_hbm, v["diag"])
    for copy in [m_copy[3], *f_copy, m_copy[2], *x_copy, m_copy[1], m_copy[0], diag_copy]:
        copy.start()

    barrier = pltpu.get_barrier_semaphore()
    for device in [sibling, *x_peer[1:], *a_peer[1:], *b_peer[1:]]:
        pl.semaphore_signal(barrier, inc=1, device_id=device, device_id_type=MESH)

    @pl.when(jnp.logical_not(stays))
    def _():
        pl.semaphore_signal(barrier, inc=1, device_id=source, device_id_type=MESH)

    pattern = pat_ref[...]

    def member(block):
        return jnp.max(jnp.where(pattern == block, 1.0, 0.0), axis=1, keepdims=True)

    inside = [member(row * 8 + b) for b in range(8)]
    inside_placed = member(row * 8 + col // 2)
    inside_summed = member(col * 4 + row // 2)

    def prep(p):
        m_copy[p].wait()
        for b in range(8):
            block = v["m32"][p, b * W:(b + 1) * W, :] * inside[b][p:p + 1, :]
            high, low = split(block.T)
            v["mh"][p % 2, :, b * W:(b + 1) * W] = high
            v["ml"][p % 2, :, b * W:(b + 1) * W] = low

    def prep_placed(p):
        rows = v["m32"][p, pl.ds(pl.multiple_of(col * 128, 128), 128), :]
        high, low = split((rows * inside_placed[p:p + 1, :]).T)
        v["oh"][p], v["ol"][p] = high, low

    def prep_cross():
        for copy in x_copy:
            copy.wait()
        for i in range(len(PAIRS)):
            block = v["x32"][i]
            v["xh"][i], v["xl"][i] = split(block)
            v["xth"][i], v["xtl"][i] = split(block.T)

    def cross(j, k):
        return v["xh"][AT[j, k]], v["xl"][AT[j, k]]

    def cross_t(j, k):
        return v["xth"][AT[j, k]], v["xtl"][AT[j, k]]

    sib_copy, r1_copy, r2_copy, place_copy = {}, {}, {}, {}

    def tile(p, t):
        if p == 3:
            f_copy[t].wait()
            v["fh"][t], v["fl"][t] = split(v["f32"][t])
        d = dot3((v["mh"][p % 2], v["ml"][p % 2]), (v["fh"][t], v["fl"][t]))
        v["part"][p, t, 0] = d[:, :128]
        v["part"][p, t, 1] = d[:, 128:]
        if p == 3 and t == 0:
            pl.semaphore_wait(barrier, jnp.where(stays, 10, 11))

        sib_copy[p, t] = send(v["part"].at[p, t, 1 - core], v["sib"].at[p, t], sibling)

    def handle(p, t):
        sib_copy[p, t].wait_recv()
        chip = v["chip"].at[p, t]
        chip[...] = v["part"][p, t, core] + v["sib"][p, t]
        if t == 0:
            r1_copy[p, 0] = send(chip.at[:128], v["r1"].at[p, 0], x_peer[1])
            r1_copy[p, 1] = send(chip.at[128:], v["r1"].at[p, 1], x_peer[3])
        if t == 1:
            r2_copy[p, 1] = send(chip.at[128:], v["r2"].at[p, 0, 128:], x_peer[1])
        if t == 2:
            r2_copy[p, 2] = send(chip.at[:128], v["r2"].at[p, 1, :128], x_peer[3])

    def combine(p):
        r1_copy[p, 0].wait_recv()
        chip = v["chip"].at[p, 1, :128]
        chip[...] += v["r1"][p, 0]
        r2_copy[p, 0] = send(chip, v["r2"].at[p, 0, :128], x_peer[1])
        r1_copy[p, 1].wait_recv()
        chip = v["chip"].at[p, 2, 128:]
        chip[...] += v["r1"][p, 1]
        r2_copy[p, 3] = send(chip, v["r2"].at[p, 1, 128:], x_peer[3])

    def final(p):
        for i in range(4):
            r2_copy[p, i].wait_recv()
        d = (v["chip"][p, 3] + v["r2"][p, 0] + v["r2"][p, 1]).T
        for j in range(p + 1, PANELS):
            d = d + dot3((v["ch"][j], v["cl"][j]), cross(j, p))
        c = -inside_summed[p:p + 1, :] * d
        v["cols"][p] = c
        if p > 0:
            v["ch"][p], v["cl"][p] = split(c)
        copy = remote(v["cols"].at[p], v["placed"].at[p], place)
        place_copy[p] = copy

        @pl.when(jnp.logical_not(stays))
        def _():
            copy.start()

        @pl.when(stays)
        def _():
            v["placed"][p] = v["cols"][p]

        def finish():
            @pl.when(jnp.logical_not(stays))
            def _():
                copy.wait_send()

        pending.append(finish)

    core_copy, a_copy, b_copy, gx_copy, back = {}, {}, {}, {}, {}
    out_copy = []

    def gram(p):
        @pl.when(jnp.logical_not(stays))
        def _():
            place_copy[p].wait_recv()

        out = local(v["placed"].at[p], cols_hbm.at[p])
        out.start()
        out_copy.append(out)
        c = split(v["placed"][p])
        for k in range(p + 1):
            value = dot3((v["oh"][k], v["ol"][k]), c)
            v[f"g{p}"][:, :, :, k] = value.reshape(2, 4, 4, 8, W)
        core_copy[p] = send(v[f"g{p}"].at[1 - core], v[f"gs{p}"], sibling)

    def reduce_a(p):
        core_copy[p].wait_recv()
        g = v[f"g{p}"].at[core]
        g[...] += v[f"gs{p}"][...]
        for s in range(1, 4):
            a_copy[p, s] = send(g.at[(a_me + s) % 4], v[f"ga{p}"].at[s - 1], a_peer[s])

    def reduce_b(p):
        g = v[f"g{p}"].at[core, a_me]
        for s in range(1, 4):
            a_copy[p, s].wait_recv()
        g[...] += v[f"ga{p}"][0] + v[f"ga{p}"][1] + v[f"ga{p}"][2]
        for s in range(1, 4):
            b_copy[p, s] = send(g.at[(b_me + s) % 4], v[f"gb{p}"].at[s - 1], b_peer[s])

    def reduce_x(p):
        for s in range(1, 4):
            b_copy[p, s].wait_recv()
        gb, gx = v[f"gb{p}"], v[f"gx{p}"]
        gx[x] = v[f"g{p}"][core, a_me, b_me] + gb[0] + gb[1] + gb[2]
        for s in range(1, 4):
            gx_copy[p, s] = send(gx.at[x], gx.at[x], x_peer[s])

    def gather_b(p):
        for s in range(1, 4):
            gx_copy[p, s].wait_recv()
        gx, res = v[f"gx{p}"], v[f"res{p}"].at[core, a_me, b_me]
        res[...] = (gx[0] + gx[1]) + (gx[2] + gx[3])
        for s in range(1, 4):
            back[p, "b", s] = send(res, res, b_peer[s])

    def gather_a(p):
        for s in range(1, 4):
            back[p, "b", s].wait_recv()
        res = v[f"res{p}"].at[core, a_me]
        for s in range(1, 4):
            back[p, "a", s] = send(res, res, a_peer[s])

    def gather_core(p):
        for s in range(1, 4):
            back[p, "a", s].wait_recv()
        res = v[f"res{p}"].at[core]
        back[p, "core"] = send(res, res, sibling)

    def put(j, k):
        copy = local(v["inv"].at[j, k], inv_hbm.at[j, k])
        copy.start()
        out_copy.append(copy)

    def block(p, k):
        return v[f"res{p}"][:, :, :, k].reshape(W, W)

    def cross_inverse(k):
        later = list(range(k + 1, PANELS))
        total = v["diag"][k]
        for j in later:
            running = block(j, k)
            for i in later:
                right = v["invt"][j] if i == j else v["inv"][i, j]
                running = running + dot3(cross_t(i, k), split(right))
            v["inv"][k, j] = -running
            v["inv"][j, k] = -running.T
            total = total + dot3(cross_t(j, k), split(running.T))
            put(k, j)
            put(j, k)
        v["pre"][...] = total

    def diagonal(k):
        back[k, "core"].wait_recv()
        value = v["pre"][...] - block(k, k)
        v["inv"][k, k] = value
        put(k, k)
        if k > 0:
            v["invt"][k] = value.T
            cross_inverse(k - 1)

    events = []

    def event(time, step, *args):
        events.append((time, len(events), step, args))

    step_us = 0.9
    for p in reversed(range(PANELS)):
        begin = 2.0 + (3 - p) * 4 * step_us
        event(begin - (0.5 if p == 3 else 1.5 * step_us), prep, p)
        for t in range(4):
            event(begin + t * step_us, tile, p, t)
            event(begin + (t + 2) * step_us + 0.3, handle, p, t)
        event(begin + 5 * step_us + 0.4, combine, p)
        when = 11.0 + (3 - p) * 4.5
        event(when, final, p)
        event(when + 2.0, gram, p)
        event(when + 3.5, reduce_a, p)
        event(when + 5.5, reduce_b, p)
        event(when + 7.0, reduce_x, p)
        event(when + 8.2, gather_b, p)
        event(when + 9.5, gather_a, p)
        event(when + 11.5, gather_core, p)
        event(when + 12.5, diagonal, p)
    event(7.5, prep_cross)
    for p in range(PANELS):
        event(12.5 + 0.1 * p, prep_placed, p)

    def prep_diag():
        diag_copy.wait()
        v["pre"][...] = v["diag"][3]

    event(12.9, prep_diag)
    for time, _, step, args in sorted(events, key=lambda e: (e[0], e[1])):
        step(*args)
    for finish in pending:
        finish()
    for copy in out_copy:
        copy.wait()


def shards(front_inverse, panel_front, panel_cross, diag_inverse, pattern):
    s = scratch()
    hbm = pl.BlockSpec(memory_space=pl.ANY)

    def body(*refs):
        kernel(s.names, *refs)

    return pl.pallas_call(
        body,
        out_shape=(
            jax.ShapeDtypeStruct((PANELS, 128, W), F32),
            jax.ShapeDtypeStruct((PANELS, PANELS, W, W), F32),
        ),
        in_specs=[hbm] * 4 + [pl.BlockSpec(memory_space=pltpu.VMEM)],
        out_specs=(hbm, hbm),
        scratch_shapes=s.shapes + [
            pltpu.SemaphoreType.DMA((REMOTE,)),
            pltpu.SemaphoreType.DMA((REMOTE,)),
            pltpu.SemaphoreType.DMA((LOCAL,)),
        ],
        compiler_params=pltpu.CompilerParams(
            collective_id=0, has_side_effects=True, vmem_limit_bytes=62 * 2**20
        ),
        cost_estimate=pl.CostEstimate(
            flops=3 * 2 * 2048 * 1024 * 1024, bytes_accessed=22 * 2**20, transcendentals=0
        ),
    )(front_inverse, panel_front, panel_cross, diag_inverse, pattern)


def solution(mesh):
    in_specs = (P("row", "col"), P(None, "row", None), P(), P(), P())
    out_specs = (P(None, ("row", "col"), None), P())
    return jax.shard_map(shards, mesh=mesh, in_specs=in_specs, out_specs=out_specs, check_vma=False)
```

time: 313 us -> 122 us (0.39)
  waiting for transfers between devices: 197 us -> 0 us
  Pallas kernels: 0 us -> 115 us
  matrix products: 52.5 us -> 0 us
  other arithmetic: 16.7 us -> 0 us
  between operations: 17.1 us -> 0.64 us
  starting transfers between devices: 11.6 us -> 0 us
  local copies, waits for them, and re-layouts: 16.6 us -> 6.46 us
    psum x1 -> x0, waiting for transfers between devices: 140 us -> none  [shards(): lax.psum(jnp.stack([inner(columns[j], own_panel[k]) for j, k in pairs]),...]
    pallas_call x0 -> x1, Pallas kernels: none -> 115 us  [shards(): pl.pallas_call(body, out_shape=(jax.ShapeDtypeStruct((PANELS, 128, W), F3...]
    dot_general x37 -> x0, matrix products: 52.5 us -> none  [the longest x20 26.5 us: product(): jnp.dot(left, right, precision=HIGH, preferred_element_type=jnp.float32)]
    reduce_scatter x1 -> x0, waiting for transfers between devices: 45.1 us -> none  [shards(): direct = lax.psum_scatter(partial, 'row', scatter_dimension=1, tiled=True)]
    ppermute x2 -> x0, waiting for transfers between devices: 12.5 us -> none  [the longest x1 12.5 us: shards(): lax.ppermute(jnp.stack(columns), ('row', 'col'), back)]
    ppermute x2 -> x0, starting transfers between devices: 11.5 us -> none  [the longest x1 7.08 us: shards(): own_panel = lax.ppermute(own_panel, ('row', 'col'), placed)]
    another operation x9 -> x0, other arithmetic: 9.54 us -> none  [the longest x5 5.86 us: shards(): jnp.stack([jnp.stack([table[j, k] for k in range(panels)]) for j in range...]
    mul x2 -> x0, other arithmetic: 5.15 us -> none  [the longest x1 4.24 us: shards(): masked = panel_front * member[:, :, None]]
  transfers between devices with their start and end apart: 4 -> 0, of which waited for: 3 -> 0; matrix products, arithmetic and copies ran while one was open for 5% -> 0% of each run, Pallas kernels for 0% -> 0%
where the time goes in v2:
time: 122 us
  Pallas kernels  115 us (94%)
  local copies, waits for them, and re-layouts  6.46 us (5%)
    pallas_call x1, Pallas kernels, shards(): pl.pallas_call(body, out_shape=(jax.ShapeDtypeStruct((PANELS, 128, W), F3...  115 us
    unnamed x2, local copies, waits for them, and re-layouts  6.46 us

profile of v2, /device:TPU:1, one launch (start us, length us, event | category | flops | bytes accessed | tf_op | source)
XLA Modules:
  0.0 121.8 jit_solution(2974438242524707322)
XLA Ops:
  0.6 114.7 %shard_map.68 = (f32[4,128,256]{2,1,0:T(8,128)}, f32[4,4,256,256]{3,2,1,0:T(8,128)}) custom-call(f32[2048,1024]{1,0:T(8,128)} %refs_0_.1, f32[4,2048,256]{2,1,0:T(8,128)} %refs_1_.1, f32[4,4,256,256]{3,2,1,0:T(8,128)} %refs_2_.1, f32[4,256,256]{2,1,0:T(8,128)} %refs_3_.1, s32[4,40]{1,0:T(4,128)} %refs_4_.1), custom_call_target="tpu_custom_call" | custom-call | flops 12884901888 | bytes 23068672 | tf_op jit(solution)/shard_map/pallas_call | solution.py:380
  115.4 1.9 %copy.9 = f32[4,128,256]{2,1,0:T(8,128)} copy(f32[4,128,256]{2,1,0:T(8,128)} %get-tuple-element.4) | data formatting | bytes 1048576
  117.2 4.6 %copy.10 = f32[4,4,256,256]{3,2,1,0:T(8,128)} copy(f32[4,4,256,256]{3,2,1,0:T(8,128)} %get-tuple-element.5) | data formatting | bytes 8388608

commit v3 on v2

--- a/solution.py
+++ b/solution.py
@@ -51,7 +51,9 @@
     s.add("cols", (PANELS, 128, W))
     s.add("ch", (PANELS, 128, W), BF16)
     s.add("cl", (PANELS, 128, W), BF16)
-    s.add("placed", (PANELS, 128, W))
+    s.add("own", (PANELS, 128, W))
+    s.add("midz", (PANELS, 128, W))
+    s.add("midy", (PANELS, 128, W))
     s.add("oh", (PANELS, W, 128), BF16)
     s.add("ol", (PANELS, W, 128), BF16)
     s.add("x32", (len(PAIRS), W, W))
@@ -66,17 +68,31 @@
         s.add(f"gb{p}", (3, n, 8, W))
         s.add(f"gx{p}", (4, n, 8, W))
         s.add(f"res{p}", (2, 4, 4, n, 8, W))
-    s.add("inv", (PANELS, PANELS, W, W))
     s.add("invt", (PANELS, W, W))
     s.add("pre", (W, W))
     return s
 
 
-REMOTE = 128
+REMOTE = 192
+VMEM_LIMIT = 58 * 2**20
+ORDER = [
+    ("prep", 3), ("tile", 3, 0), ("tile", 3, 1), ("tile", 3, 2), ("handle", 3, 0), ("tile", 3, 3),
+    ("handle", 3, 2), ("tile", 2, 0), ("tile", 2, 1), ("handle", 3, 1), ("handle", 2, 0), ("tile", 2, 2),
+    ("tile", 2, 3), ("tile", 1, 0), ("combine", 3), ("handle", 2, 2), ("cross",), ("diag",), ("handle", 2, 1),
+    ("handle", 1, 0), ("own", 2), ("tile", 1, 1), ("own", 1), ("tile", 1, 2), ("combine", 2), ("own", 3),
+    ("handle", 3, 3), ("own", 0), ("final", 3), ("pz", 3), ("handle", 1, 1), ("tile", 1, 3), ("handle", 2, 3),
+    ("handle", 1, 2), ("combine", 1), ("ra", 3), ("tile", 0, 0), ("final", 2), ("pz", 2), ("handle", 0, 0),
+    ("py", 3), ("tile", 0, 1), ("tile", 0, 2), ("ra", 2), ("handle", 1, 3), ("handle", 0, 1), ("handle", 0, 2),
+    ("rb", 3), ("combine", 0), ("final", 1), ("pz", 1), ("py", 2), ("tile", 0, 3), ("ra", 1), ("rb", 2),
+    ("handle", 0, 3), ("rx", 3), ("final", 0), ("pz", 0), ("py", 1), ("px", 3), ("ra", 0), ("rb", 1), ("rx", 2),
+    ("gb", 3), ("py", 0), ("rx", 1), ("rb", 0), ("gb", 2), ("px", 2), ("ga", 3), ("rx", 0), ("gb", 1), ("ga", 2),
+    ("px", 0), ("gb", 0), ("gc", 3), ("ga", 1), ("ga", 0), ("settle",), ("px", 1), ("inv", 3), ("gc", 2),
+    ("gc", 1), ("inv", 2), ("gc", 0), ("inv", 1), ("inv", 0),
+]
 LOCAL = 64
 
 
-def kernel(names, f_hbm, m_hbm, x_hbm, diag_hbm, pat_ref, cols_hbm, inv_hbm, *refs):
+def kernel(names, f_hbm, m_hbm, x_hbm, diag_hbm, pat_ref, cols_out, inv_out, *refs):
     v = dict(zip(names, refs))
     send_sem, recv_sem, local_sem = refs[len(names):]
     row, col = lax.axis_index("row"), lax.axis_index("col")
@@ -91,11 +107,20 @@
     a_me, b_me = y + (z - y) * core, z + (y - z) * core
     a_peer = [at(x, y + s * (1 - core), z + s * core, core) for s in range(4)]
     b_peer = [at(x, y + s * core, z + s * (1 - core), core) for s in range(4)]
-    to = col * 8 + row
+    chunk = (x + y + z) % 4
+    to = col * 8 + 2 * chunk + core
     place = (to // 16, to % 16)
-    here = row * 16 + col
-    source = (here % 8, here // 8)
-    stays = to == here
+    stays = to == row * 16 + col
+    rows_c, rows_k = (row * 16 + col) // 8, (row * 16 + col) % 8
+    owner = at(rows_k // 2 - rows_c // 4 - rows_c % 4 + 8, rows_c // 4, rows_c % 4, rows_k % 2)
+    to_z = at(x, y, chunk % 2 * 2 + core, z // 2)
+    to_z_stays = (to_z[0] == row) & (to_z[1] == col)
+    z_was = 2 * core + (z // 2 + x + y) % 2
+    to_z_source = at(x, y, z_was, z % 2)
+    y_next = z_was % 2 * 2 + (x + y + z_was) % 4 // 2
+    to_y = at(x, y_next, z, core)
+    x_next = (col % 8 // 2 - x - 2 * core - col // 8 + 8) % 4
+    to_x = at(x_next, y, z, core)
 
     counts = {"remote": 0, "local": 0}
     pending = []
@@ -122,7 +147,7 @@
     m_copy = [local(m_hbm.at[p], v["m32"].at[p]) for p in range(PANELS)]
     f_copy = []
     for t in range(4):
-        first = pl.multiple_of((xs[t] % 4) * W, W)
+        first = pl.multiple_of(((xs[t] + y + z) % 4) * W, W)
         f_copy.append(local(f_hbm.at[:, pl.ds(first, W)], v["f32"].at[t]))
     x_copy = [local(x_hbm.at[j, k], v["x32"].at[AT[j, k]]) for j, k in PAIRS]
     diag_copy = local(diag_hbm, v["diag"])
@@ -135,7 +160,11 @@
 
     @pl.when(jnp.logical_not(stays))
     def _():
-        pl.semaphore_signal(barrier, inc=1, device_id=source, device_id_type=MESH)
+        pl.semaphore_signal(barrier, inc=1, device_id=place, device_id_type=MESH)
+
+    @pl.when(jnp.logical_not(to_z_stays))
+    def _():
+        pl.semaphore_signal(barrier, inc=1, device_id=to_z_source, device_id_type=MESH)
 
     pattern = pat_ref[...]
 
@@ -143,20 +172,43 @@
         return jnp.max(jnp.where(pattern == block, 1.0, 0.0), axis=1, keepdims=True)
 
     inside = [member(row * 8 + b) for b in range(8)]
-    inside_placed = member(row * 8 + col // 2)
-    inside_summed = member(col * 4 + row // 2)
-
-    def prep(p):
-        m_copy[p].wait()
-        for b in range(8):
+    inside_summed = member(col * 4 + chunk)
+
+    def prep(p, blocks):
+        if blocks[0] == 0:
+            m_copy[p].wait()
+        for b in blocks:
             block = v["m32"][p, b * W:(b + 1) * W, :] * inside[b][p:p + 1, :]
             high, low = split(block.T)
             v["mh"][p % 2, :, b * W:(b + 1) * W] = high
             v["ml"][p % 2, :, b * W:(b + 1) * W] = low
 
-    def prep_placed(p):
-        rows = v["m32"][p, pl.ds(pl.multiple_of(col * 128, 128), 128), :]
-        high, low = split((rows * inside_placed[p:p + 1, :]).T)
+    own_copy = {}
+
+    def enter():
+        pl.semaphore_wait(barrier, 10 + jnp.where(stays, 0, 1) + jnp.where(to_z_stays, 0, 1))
+        rows = pl.ds(pl.multiple_of(col * 128, 128), 128)
+        for p in reversed(range(PANELS)):
+            own_copy[p] = remote(m_hbm.at[p, rows], v["own"].at[p], owner)
+
+        @pl.when(jnp.logical_not(stays))
+        def _():
+            for copy in own_copy.values():
+                copy.start()
+
+        @pl.when(stays)
+        def _():
+            for p in range(PANELS):
+                copy = local(m_hbm.at[p, rows], v["own"].at[p])
+                copy.start()
+                copy.wait()
+
+    def prep_own(p):
+        @pl.when(jnp.logical_not(stays))
+        def _():
+            own_copy[p].wait()
+
+        high, low = split((v["own"][p] * inside_summed[p:p + 1, :]).T)
         v["oh"][p], v["ol"][p] = high, low
 
     def prep_cross():
@@ -174,17 +226,20 @@
         return v["xth"][AT[j, k]], v["xtl"][AT[j, k]]
 
     sib_copy, r1_copy, r2_copy, place_copy = {}, {}, {}, {}
+    core_copy, a_copy, b_copy, gx_copy, back = {}, {}, {}, {}, {}
+    last = []
 
     def tile(p, t):
         if p == 3:
             f_copy[t].wait()
             v["fh"][t], v["fl"][t] = split(v["f32"][t])
+        if p > 0:
+            prep(p - 1, (2 * t, 2 * t + 1))
         d = dot3((v["mh"][p % 2], v["ml"][p % 2]), (v["fh"][t], v["fl"][t]))
         v["part"][p, t, 0] = d[:, :128]
         v["part"][p, t, 1] = d[:, 128:]
-        if p == 3 and t == 0:
-            pl.semaphore_wait(barrier, jnp.where(stays, 10, 11))
-
+        if (p, t) == (3, 0):
+            enter()
         sib_copy[p, t] = send(v["part"].at[p, t, 1 - core], v["sib"].at[p, t], sibling)
 
     def handle(p, t):
@@ -213,46 +268,62 @@
         for i in range(4):
             r2_copy[p, i].wait_recv()
         d = (v["chip"][p, 3] + v["r2"][p, 0] + v["r2"][p, 1]).T
+        gram(p, p, split(d))
+        if p == 0:
+            core_copy[p] = send(v["g0"].at[1 - core], v["gs0"], sibling)
         for j in range(p + 1, PANELS):
             d = d + dot3((v["ch"][j], v["cl"][j]), cross(j, p))
         c = -inside_summed[p:p + 1, :] * d
         v["cols"][p] = c
         if p > 0:
-            v["ch"][p], v["cl"][p] = split(c)
-        copy = remote(v["cols"].at[p], v["placed"].at[p], place)
-        place_copy[p] = copy
-
-        @pl.when(jnp.logical_not(stays))
+            pair = split(c)
+            v["ch"][p], v["cl"][p] = pair
+            for k in range(p):
+                gram(p, k, pair)
+            core_copy[p] = send(v[f"g{p}"].at[1 - core], v[f"gs{p}"], sibling)
+
+    def move(src, dst, device, here):
+        copy, stay = remote(src, dst, device), local(src, dst)
+
+        @pl.when(jnp.logical_not(here))
         def _():
             copy.start()
 
-        @pl.when(stays)
+        @pl.when(here)
         def _():
-            v["placed"][p] = v["cols"][p]
-
-        def finish():
-            @pl.when(jnp.logical_not(stays))
+            stay.start()
+
+        def arrive():
+            @pl.when(jnp.logical_not(here))
+            def _():
+                copy.wait_recv()
+
+            @pl.when(here)
+            def _():
+                stay.wait()
+
+        def sent():
+            @pl.when(jnp.logical_not(here))
             def _():
                 copy.wait_send()
 
-        pending.append(finish)
-
-    core_copy, a_copy, b_copy, gx_copy, back = {}, {}, {}, {}, {}
-    out_copy = []
-
-    def gram(p):
-        @pl.when(jnp.logical_not(stays))
-        def _():
-            place_copy[p].wait_recv()
-
-        out = local(v["placed"].at[p], cols_hbm.at[p])
-        out.start()
-        out_copy.append(out)
-        c = split(v["placed"][p])
-        for k in range(p + 1):
-            value = dot3((v["oh"][k], v["ol"][k]), c)
-            v[f"g{p}"][:, :, :, k] = value.reshape(2, 4, 4, 8, W)
-        core_copy[p] = send(v[f"g{p}"].at[1 - core], v[f"gs{p}"], sibling)
+        last.append(sent)
+        return arrive
+
+    def place_z(p):
+        place_copy[p] = move(v["cols"].at[p], v["midz"].at[p], to_z, to_z_stays)
+
+    def place_y(p):
+        place_copy[p]()
+        place_copy[p] = move(v["midz"].at[p], v["midy"].at[p], to_y, y_next == y)
+
+    def place_x(p):
+        place_copy[p]()
+        place_copy[p] = move(v["midy"].at[p], cols_out.at[p], to_x, x_next == x)
+
+    def gram(p, k, right):
+        value = dot3((v["oh"][k], v["ol"][k]), right)
+        v[f"g{p}"][:, :, :, k] = value.reshape(2, 4, 4, 8, W)
 
     def reduce_a(p):
         core_copy[p].wait_recv()
@@ -293,15 +364,11 @@
             back[p, "a", s] = send(res, res, a_peer[s])
 
     def gather_core(p):
-        for s in range(1, 4):
-            back[p, "a", s].wait_recv()
+        for key, copy in back.items():
+            if key[:2] == (p, "a"):
+                copy.wait_recv()
         res = v[f"res{p}"].at[core]
         back[p, "core"] = send(res, res, sibling)
-
-    def put(j, k):
-        copy = local(v["inv"].at[j, k], inv_hbm.at[j, k])
-        copy.start()
-        out_copy.append(copy)
 
     def block(p, k):
         return v[f"res{p}"][:, :, :, k].reshape(W, W)
@@ -311,92 +378,91 @@
         total = v["diag"][k]
         for j in later:
             running = block(j, k)
+            total = total + dot3(split(running), cross(j, k))
             for i in later:
-                right = v["invt"][j] if i == j else v["inv"][i, j]
+                right = v["invt"][j] if i == j else inv_out[i, j]
                 running = running + dot3(cross_t(i, k), split(right))
-            v["inv"][k, j] = -running
-            v["inv"][j, k] = -running.T
+            inv_out[k, j] = -running
+            inv_out[j, k] = -running.T
             total = total + dot3(cross_t(j, k), split(running.T))
-            put(k, j)
-            put(j, k)
         v["pre"][...] = total
 
     def diagonal(k):
         back[k, "core"].wait_recv()
-        value = v["pre"][...] - block(k, k)
-        v["inv"][k, k] = value
-        put(k, k)
+        value = v["pre"][...] + block(k, k)
+        inv_out[k, k] = value
         if k > 0:
             v["invt"][k] = value.T
             cross_inverse(k - 1)
 
-    events = []
-
-    def event(time, step, *args):
-        events.append((time, len(events), step, args))
-
-    step_us = 0.9
-    for p in reversed(range(PANELS)):
-        begin = 2.0 + (3 - p) * 4 * step_us
-        event(begin - (0.5 if p == 3 else 1.5 * step_us), prep, p)
-        for t in range(4):
-            event(begin + t * step_us, tile, p, t)
-            event(begin + (t + 2) * step_us + 0.3, handle, p, t)
-        event(begin + 5 * step_us + 0.4, combine, p)
-        when = 11.0 + (3 - p) * 4.5
-        event(when, final, p)
-        event(when + 2.0, gram, p)
-        event(when + 3.5, reduce_a, p)
-        event(when + 5.5, reduce_b, p)
-        event(when + 7.0, reduce_x, p)
-        event(when + 8.2, gather_b, p)
-        event(when + 9.5, gather_a, p)
-        event(when + 11.5, gather_core, p)
-        event(when + 12.5, diagonal, p)
-    event(7.5, prep_cross)
-    for p in range(PANELS):
-        event(12.5 + 0.1 * p, prep_placed, p)
-
-    def prep_diag():
+    def start_diag():
         diag_copy.wait()
         v["pre"][...] = v["diag"][3]
 
-    event(12.9, prep_diag)
-    for time, _, step, args in sorted(events, key=lambda e: (e[0], e[1])):
-        step(*args)
-    for finish in pending:
+    def settle():
+        for finish in pending:
+            finish()
+        pending.clear()
+
+    steps = {
+        "prep": lambda p: prep(p, range(8)), "tile": tile, "handle": handle, "combine": combine,
+        "own": prep_own, "cross": prep_cross, "diag": start_diag, "final": final, "ra": reduce_a, "rb": reduce_b,
+        "rx": reduce_x, "gb": gather_b, "ga": gather_a, "gc": gather_core, "inv": diagonal, "pz": place_z,
+        "py": place_y, "px": place_x, "settle": settle,
+    }
+    for name, *where in ORDER:
+        steps[name](*where)
+    settle()
+    for p in range(PANELS):
+        place_copy[p]()
+    for finish in last:
         finish()
-    for copy in out_copy:
+
+
+def copy_kernel(cols_in, inv_in, cols_hbm, inv_hbm, sem):
+    copies = [
+        pltpu.make_async_copy(cols_in, cols_hbm, sem.at[0]),
+        *[pltpu.make_async_copy(inv_in.at[k], inv_hbm.at[k], sem.at[1 + k]) for k in range(PANELS)],
+    ]
+    for copy in copies:
+        copy.start()
+    for copy in copies:
         copy.wait()
 
 
 def shards(front_inverse, panel_front, panel_cross, diag_inverse, pattern):
     s = scratch()
-    hbm = pl.BlockSpec(memory_space=pl.ANY)
+    hbm, vmem = pl.BlockSpec(memory_space=pl.ANY), pl.BlockSpec(memory_space=pltpu.VMEM)
+    shapes = (PANELS, 128, W), (PANELS, PANELS, W, W)
 
     def body(*refs):
         kernel(s.names, *refs)
 
-    return pl.pallas_call(
+    held = pl.pallas_call(
         body,
-        out_shape=(
-            jax.ShapeDtypeStruct((PANELS, 128, W), F32),
-            jax.ShapeDtypeStruct((PANELS, PANELS, W, W), F32),
-        ),
-        in_specs=[hbm] * 4 + [pl.BlockSpec(memory_space=pltpu.VMEM)],
-        out_specs=(hbm, hbm),
+        out_shape=tuple(pltpu.VMEM(shape, F32) for shape in shapes),
+        in_specs=[hbm] * 4 + [vmem],
+        out_specs=(vmem, vmem),
         scratch_shapes=s.shapes + [
             pltpu.SemaphoreType.DMA((REMOTE,)),
             pltpu.SemaphoreType.DMA((REMOTE,)),
             pltpu.SemaphoreType.DMA((LOCAL,)),
         ],
         compiler_params=pltpu.CompilerParams(
-            collective_id=0, has_side_effects=True, vmem_limit_bytes=62 * 2**20
+            collective_id=0, has_side_effects=True, vmem_limit_bytes=VMEM_LIMIT
         ),
         cost_estimate=pl.CostEstimate(
             flops=3 * 2 * 2048 * 1024 * 1024, bytes_accessed=22 * 2**20, transcendentals=0
         ),
     )(front_inverse, panel_front, panel_cross, diag_inverse, pattern)
+    return pl.pallas_call(
+        copy_kernel,
+        out_shape=tuple(jax.ShapeDtypeStruct(shape, F32) for shape in shapes),
+        in_specs=[vmem, vmem],
+        out_specs=(hbm, hbm),
+        scratch_shapes=[pltpu.SemaphoreType.DMA((1 + PANELS,))],
+        compiler_params=pltpu.CompilerParams(vmem_limit_bytes=8 * 2**20),
+    )(*held)
 
 
 def solution(mesh):

time: 122 us -> 83.9 us (0.69)
  Pallas kernels: 115 us -> 82.9 us
  local copies, waits for them, and re-layouts: 6.46 us -> 0 us
    pallas_call x1 -> x2, Pallas kernels: 115 us -> 82.9 us  [the longest x1 80.6 us: shards(): pl.pallas_call(body, out_shape=tuple((pltpu.VMEM(shape, F32) for shape in...]
    unnamed x2 -> x0, local copies, waits for them, and re-layouts: 6.46 us -> none
where the time goes in v3:
time: 83.9 us; the launch traced here: 83.7 us
  Pallas kernels  82.9 us (99%)
    pallas_call x1, Pallas kernels, shards(): pl.pallas_call(body, out_shape=tuple((pltpu.VMEM(shape, F32) for shape in...  80.6 us
    pallas_call x1, Pallas kernels, shards(): pl.pallas_call(copy_kernel, out_shape=tuple((jax.ShapeDtypeStruct(shape,...  2.22 us

profile of v3, /device:TPU:1, one launch (start us, length us, event | category | flops | bytes accessed | tf_op | source)
XLA Modules:
  0.0 83.7 jit_solution(15045878613830557664)
XLA Ops:
  0.6 80.6 %shard_map.68 = (f32[4,128,256]{2,1,0:T(8,128)S(1)}, f32[4,4,256,256]{3,2,1,0:T(8,128)S(1)}) custom-call(f32[2048,1024]{1,0:T(8,128)} %refs_0_.1, f32[4,2048,256]{2,1,0:T(8,128)} %refs_1_.1, f32[4,4,256,256]{3,2,1,0:T(8,128)} %refs_2_.1, f32[4,256,256]{2,1,0:T(8,128)} %refs_3_.1, s32[4,40]{1,0:T(4,128)} %refs_4_.1), custom_call_target="tpu_custom_call" | custom-call | flops 12884901888 | bytes 23068672 | tf_op jit(solution)/shard_map/pallas_call | solution.py:441
  81.3 2.2 %shard_map.69 = (f32[4,128,256]{2,1,0:T(8,128)}, f32[4,4,256,256]{3,2,1,0:T(8,128)}) custom-call(f32[4,128,256]{2,1,0:T(8,128)S(1)} %get-tuple-element.4.cols_in, f32[4,4,256,256]{3,2,1,0:T(8,128)S(1)} %get-tuple-element.5.inv_in), custom_call_target="tpu_custom_call" | custom-call | tf_op jit(solution)/shard_map/pallas_call | solution.py:458

commit v4 on v3

--- a/solution.py
+++ b/solution.py
@@ -41,8 +41,8 @@
     s.add("f32", (4, 2048, W))
     s.add("fh", (4, 2048, W), BF16)
     s.add("fl", (4, 2048, W), BF16)
-    s.add("mh", (2, W, 2048), BF16)
-    s.add("ml", (2, W, 2048), BF16)
+    s.add("mh", (W, 2048), BF16)
+    s.add("ml", (W, 2048), BF16)
     s.add("part", (PANELS, 4, 2, W, 128))
     s.add("sib", (PANELS, 4, W, 128))
     s.add("chip", (PANELS, 4, W, 128))
@@ -75,26 +75,56 @@
 
 REMOTE = 192
 VMEM_LIMIT = 58 * 2**20
-ORDER = [
-    ("prep", 3), ("tile", 3, 0), ("tile", 3, 1), ("tile", 3, 2), ("handle", 3, 0), ("tile", 3, 3),
-    ("handle", 3, 2), ("tile", 2, 0), ("tile", 2, 1), ("handle", 3, 1), ("handle", 2, 0), ("tile", 2, 2),
-    ("tile", 2, 3), ("tile", 1, 0), ("combine", 3), ("handle", 2, 2), ("cross",), ("diag",), ("handle", 2, 1),
-    ("handle", 1, 0), ("own", 2), ("tile", 1, 1), ("own", 1), ("tile", 1, 2), ("combine", 2), ("own", 3),
-    ("handle", 3, 3), ("own", 0), ("final", 3), ("pz", 3), ("handle", 1, 1), ("tile", 1, 3), ("handle", 2, 3),
-    ("handle", 1, 2), ("combine", 1), ("ra", 3), ("tile", 0, 0), ("final", 2), ("pz", 2), ("handle", 0, 0),
-    ("py", 3), ("tile", 0, 1), ("tile", 0, 2), ("ra", 2), ("handle", 1, 3), ("handle", 0, 1), ("handle", 0, 2),
-    ("rb", 3), ("combine", 0), ("final", 1), ("pz", 1), ("py", 2), ("tile", 0, 3), ("ra", 1), ("rb", 2),
-    ("handle", 0, 3), ("rx", 3), ("final", 0), ("pz", 0), ("py", 1), ("px", 3), ("ra", 0), ("rb", 1), ("rx", 2),
-    ("gb", 3), ("py", 0), ("rx", 1), ("rb", 0), ("gb", 2), ("px", 2), ("ga", 3), ("rx", 0), ("gb", 1), ("ga", 2),
-    ("px", 0), ("gb", 0), ("gc", 3), ("ga", 1), ("ga", 0), ("settle",), ("px", 1), ("inv", 3), ("gc", 2),
-    ("gc", 1), ("inv", 2), ("gc", 0), ("inv", 1), ("inv", 0),
+BETWEEN = [
+    [],
+    [],
+    [
+        ("handle", 3, 0),
+    ],
+    [
+        ("handle", 3, 2),
+    ],
+    [],
+    [
+        ("handle", 3, 1), ("handle", 2, 0),
+    ],
+    [],
+    [],
+    [
+        ("combine", 3), ("handle", 2, 2), ("cross",), ("diag",), ("handle", 2, 1), ("handle", 1, 0),
+        ("own", 2),
+    ],
+    [
+        ("own", 1),
+    ],
+    [
+        ("combine", 2), ("own", 3), ("handle", 3, 3), ("own", 0), ("final", 3), ("pz", 3), ("handle", 1, 1),
+    ],
+    [
+        ("handle", 2, 3), ("handle", 1, 2), ("combine", 1), ("ra", 3),
+    ],
+    [
+        ("final", 2), ("pz", 2), ("handle", 0, 0), ("py", 3),
+    ],
+    [],
+    [
+        ("ra", 2), ("handle", 1, 3), ("handle", 0, 1), ("handle", 0, 2), ("rb", 3), ("combine", 0),
+        ("final", 1), ("pz", 1), ("py", 2),
+    ],
+    [],
+]
+AFTER = [
+    ("ra", 1), ("rb", 2), ("handle", 0, 3), ("rx", 3), ("final", 0), ("pz", 0), ("py", 1), ("px", 3),
+    ("ra", 0), ("rb", 1), ("rx", 2), ("gb", 3), ("py", 0), ("rx", 1), ("rb", 0), ("gb", 2), ("px", 2),
+    ("ga", 3), ("rx", 0), ("gb", 1), ("ga", 2), ("px", 0), ("gb", 0), ("gc", 3), ("ga", 1), ("ga", 0),
+    ("settle",), ("px", 1), ("inv", 3), ("gc", 2), ("gc", 1), ("inv", 2), ("gc", 0), ("inv", 1), ("inv", 0),
 ]
 LOCAL = 64
 
 
 def kernel(names, f_hbm, m_hbm, x_hbm, diag_hbm, pat_ref, cols_out, inv_out, *refs):
     v = dict(zip(names, refs))
-    send_sem, recv_sem, local_sem = refs[len(names):]
+    send_sem, recv_sem, local_sem, sib_send_sem, sib_recv_sem = refs[len(names):]
     row, col = lax.axis_index("row"), lax.axis_index("col")
     x, core = row // 2, row % 2
     y, z = col // 4, col % 4
@@ -122,35 +152,68 @@
     x_next = (col % 8 // 2 - x - 2 * core - col // 8 + 8) % 4
     to_x = at(x_next, y, z, core)
 
+    other = 1 - core
+    a_at = [(a_me + s) % 4 for s in range(4)]
+    b_at = [(b_me + s) % 4 for s in range(4)]
+    own_rows = pl.ds(pl.multiple_of(col * 128, 128), 128)
+    away, away_z, y_here, x_here = jnp.logical_not(stays), jnp.logical_not(to_z_stays), y_next == y, x_next == x
+    y_away, x_away = jnp.logical_not(y_here), jnp.logical_not(x_here)
+
     counts = {"remote": 0, "local": 0}
     pending = []
 
-    def remote(src, dst, device):
-        i = counts["remote"]
-        counts["remote"] += 1
-        return pltpu.make_async_remote_copy(
-            src, dst, send_sem.at[i], recv_sem.at[i], device_id=device, device_id_type=MESH
-        )
-
-    def local(src, dst):
-        i = counts["local"]
-        counts["local"] += 1
-        return pltpu.make_async_copy(src, dst, local_sem.at[i])
+    class Remote:
+        def __init__(self, src, dst, device):
+            self.what = src, dst, counts["remote"], device
+            counts["remote"] += 1
+
+        def copy(self):
+            src, dst, i, device = self.what
+            return pltpu.make_async_remote_copy(
+                src(), dst(), send_sem.at[i], recv_sem.at[i], device_id=device, device_id_type=MESH
+            )
+
+        def start(self):
+            self.copy().start()
+
+        def wait_recv(self):
+            self.copy().wait_recv()
+
+        def wait_send(self):
+            self.copy().wait_send()
+
+    class Local:
+        def __init__(self, src, dst):
+            self.what = src, dst, counts["local"]
+            counts["local"] += 1
+
+        def copy(self):
+            src, dst, i = self.what
+            return pltpu.make_async_copy(src(), dst(), local_sem.at[i])
+
+        def start(self):
+            self.copy().start()
+
+        def wait(self):
+            self.copy().wait()
 
     def send(src, dst, device):
-        copy = remote(src, dst, device)
+        copy = Remote(src, dst, device)
         copy.start()
         pending.append(copy.wait_send)
         return copy
 
+    def part_of(name, *index):
+        return lambda: v[name].at[index]
+
     xs = [x + 2, x + 1, x + 3, x]
-    m_copy = [local(m_hbm.at[p], v["m32"].at[p]) for p in range(PANELS)]
+    m_copy = [Local(lambda p=p: m_hbm.at[p], part_of("m32", p)) for p in range(PANELS)]
     f_copy = []
     for t in range(4):
         first = pl.multiple_of(((xs[t] + y + z) % 4) * W, W)
-        f_copy.append(local(f_hbm.at[:, pl.ds(first, W)], v["f32"].at[t]))
-    x_copy = [local(x_hbm.at[j, k], v["x32"].at[AT[j, k]]) for j, k in PAIRS]
-    diag_copy = local(diag_hbm, v["diag"])
+        f_copy.append(Local(lambda first=first: f_hbm.at[:, pl.ds(first, W)], part_of("f32", t)))
+    x_copy = [Local(lambda j=j, k=k: x_hbm.at[j, k], part_of("x32", AT[j, k])) for j, k in PAIRS]
+    diag_copy = Local(lambda: diag_hbm, lambda: v["diag"])
     for copy in [m_copy[3], *f_copy, m_copy[2], *x_copy, m_copy[1], m_copy[0], diag_copy]:
         copy.start()
 
@@ -174,24 +237,24 @@
     inside = [member(row * 8 + b) for b in range(8)]
     inside_summed = member(col * 4 + chunk)
 
-    def prep(p, blocks):
-        if blocks[0] == 0:
-            m_copy[p].wait()
-        for b in blocks:
-            block = v["m32"][p, b * W:(b + 1) * W, :] * inside[b][p:p + 1, :]
-            high, low = split(block.T)
-            v["mh"][p % 2, :, b * W:(b + 1) * W] = high
-            v["ml"][p % 2, :, b * W:(b + 1) * W] = low
+    def prep(p):
+        pltpu.make_async_copy(m_hbm.at[p], v["m32"].at[p], local_sem.at[p]).wait()
+        for b in range(8):
+            keep = inside[b][3:, :]
+            for k in range(PANELS - 1):
+                keep = jnp.where(p == k, inside[b][k:k + 1, :], keep)
+            high, low = split((v["m32"][p, b * W:(b + 1) * W, :] * keep).T)
+            v["mh"][:, b * W:(b + 1) * W] = high
+            v["ml"][:, b * W:(b + 1) * W] = low
 
     own_copy = {}
 
     def enter():
         pl.semaphore_wait(barrier, 10 + jnp.where(stays, 0, 1) + jnp.where(to_z_stays, 0, 1))
-        rows = pl.ds(pl.multiple_of(col * 128, 128), 128)
         for p in reversed(range(PANELS)):
-            own_copy[p] = remote(m_hbm.at[p, rows], v["own"].at[p], owner)
-
-        @pl.when(jnp.logical_not(stays))
+            own_copy[p] = Remote(lambda p=p: m_hbm.at[p, own_rows], part_of("own", p), owner)
+
+        @pl.when(away)
         def _():
             for copy in own_copy.values():
                 copy.start()
@@ -199,14 +262,15 @@
         @pl.when(stays)
         def _():
             for p in range(PANELS):
-                copy = local(m_hbm.at[p, rows], v["own"].at[p])
+                copy = Local(lambda p=p: m_hbm.at[p, own_rows], part_of("own", p))
                 copy.start()
                 copy.wait()
 
     def prep_own(p):
-        @pl.when(jnp.logical_not(stays))
-        def _():
-            own_copy[p].wait()
+        @pl.when(away)
+        def _():
+            own_copy[p].wait_recv()
+            own_copy[p].wait_send()
 
         high, low = split((v["own"][p] * inside_summed[p:p + 1, :]).T)
         v["oh"][p], v["ol"][p] = high, low
@@ -225,44 +289,60 @@
     def cross_t(j, k):
         return v["xth"][AT[j, k]], v["xtl"][AT[j, k]]
 
-    sib_copy, r1_copy, r2_copy, place_copy = {}, {}, {}, {}
+    r1_copy, r2_copy, place_copy = {}, {}, {}
     core_copy, a_copy, b_copy, gx_copy, back = {}, {}, {}, {}, {}
     last = []
 
-    def tile(p, t):
-        if p == 3:
-            f_copy[t].wait()
+    def sib_copy(p, t):
+        i = (3 - p) * 4 + t
+        return pltpu.make_async_remote_copy(
+            v["part"].at[p, t, other], v["sib"].at[p, t], sib_send_sem.at[i], sib_recv_sem.at[i],
+            device_id=sibling, device_id_type=MESH,
+        )
+
+    def tile(step):
+        p, t = 3 - step // 4, step % 4
+
+        @pl.when(t == 0)
+        def _():
+            prep(p)
+
+        @pl.when(step < 4)
+        def _():
+            pltpu.make_async_copy(v["f32"].at[t], v["f32"].at[t], local_sem.at[PANELS + t]).wait()
             v["fh"][t], v["fl"][t] = split(v["f32"][t])
-        if p > 0:
-            prep(p - 1, (2 * t, 2 * t + 1))
-        d = dot3((v["mh"][p % 2], v["ml"][p % 2]), (v["fh"][t], v["fl"][t]))
+
+        d = dot3((v["mh"][...], v["ml"][...]), (v["fh"][t], v["fl"][t]))
         v["part"][p, t, 0] = d[:, :128]
         v["part"][p, t, 1] = d[:, 128:]
-        if (p, t) == (3, 0):
+
+        @pl.when(step == 0)
+        def _():
             enter()
-        sib_copy[p, t] = send(v["part"].at[p, t, 1 - core], v["sib"].at[p, t], sibling)
+
+        sib_copy(p, t).start()
 
     def handle(p, t):
-        sib_copy[p, t].wait_recv()
+        sib_copy(p, t).wait_recv()
         chip = v["chip"].at[p, t]
         chip[...] = v["part"][p, t, core] + v["sib"][p, t]
         if t == 0:
-            r1_copy[p, 0] = send(chip.at[:128], v["r1"].at[p, 0], x_peer[1])
-            r1_copy[p, 1] = send(chip.at[128:], v["r1"].at[p, 1], x_peer[3])
+            r1_copy[p, 0] = send(part_of("chip", p, 0, pl.ds(0, 128)), part_of("r1", p, 0), x_peer[1])
+            r1_copy[p, 1] = send(part_of("chip", p, 0, pl.ds(128, 128)), part_of("r1", p, 1), x_peer[3])
         if t == 1:
-            r2_copy[p, 1] = send(chip.at[128:], v["r2"].at[p, 0, 128:], x_peer[1])
+            r2_copy[p, 1] = send(part_of("chip", p, 1, pl.ds(128, 128)), part_of("r2", p, 0, pl.ds(128, 128)), x_peer[1])
         if t == 2:
-            r2_copy[p, 2] = send(chip.at[:128], v["r2"].at[p, 1, :128], x_peer[3])
+            r2_copy[p, 2] = send(part_of("chip", p, 2, pl.ds(0, 128)), part_of("r2", p, 1, pl.ds(0, 128)), x_peer[3])
 
     def combine(p):
         r1_copy[p, 0].wait_recv()
         chip = v["chip"].at[p, 1, :128]
         chip[...] += v["r1"][p, 0]
-        r2_copy[p, 0] = send(chip, v["r2"].at[p, 0, :128], x_peer[1])
+        r2_copy[p, 0] = send(part_of("chip", p, 1, pl.ds(0, 128)), part_of("r2", p, 0, pl.ds(0, 128)), x_peer[1])
         r1_copy[p, 1].wait_recv()
         chip = v["chip"].at[p, 2, 128:]
         chip[...] += v["r1"][p, 1]
-        r2_copy[p, 3] = send(chip, v["r2"].at[p, 1, 128:], x_peer[3])
+        r2_copy[p, 3] = send(part_of("chip", p, 2, pl.ds(128, 128)), part_of("r2", p, 1, pl.ds(128, 128)), x_peer[3])
 
     def final(p):
         for i in range(4):
@@ -270,7 +350,7 @@
         d = (v["chip"][p, 3] + v["r2"][p, 0] + v["r2"][p, 1]).T
         gram(p, p, split(d))
         if p == 0:
-            core_copy[p] = send(v["g0"].at[1 - core], v["gs0"], sibling)
+            core_copy[p] = send(part_of("g0", other), lambda: v["gs0"], sibling)
         for j in range(p + 1, PANELS):
             d = d + dot3((v["ch"][j], v["cl"][j]), cross(j, p))
         c = -inside_summed[p:p + 1, :] * d
@@ -280,12 +360,12 @@
             v["ch"][p], v["cl"][p] = pair
             for k in range(p):
                 gram(p, k, pair)
-            core_copy[p] = send(v[f"g{p}"].at[1 - core], v[f"gs{p}"], sibling)
-
-    def move(src, dst, device, here):
-        copy, stay = remote(src, dst, device), local(src, dst)
-
-        @pl.when(jnp.logical_not(here))
+            core_copy[p] = send(part_of(f"g{p}", other), lambda: v[f"gs{p}"], sibling)
+
+    def move(src, dst, device, here, away):
+        copy, stay = Remote(src, dst, device), Local(src, dst)
+
+        @pl.when(away)
         def _():
             copy.start()
 
@@ -294,7 +374,7 @@
             stay.start()
 
         def arrive():
-            @pl.when(jnp.logical_not(here))
+            @pl.when(away)
             def _():
                 copy.wait_recv()
 
@@ -303,7 +383,7 @@
                 stay.wait()
 
         def sent():
-            @pl.when(jnp.logical_not(here))
+            @pl.when(away)
             def _():
                 copy.wait_send()
 
@@ -311,15 +391,15 @@
         return arrive
 
     def place_z(p):
-        place_copy[p] = move(v["cols"].at[p], v["midz"].at[p], to_z, to_z_stays)
+        place_copy[p] = move(part_of("cols", p), part_of("midz", p), to_z, to_z_stays, away_z)
 
     def place_y(p):
         place_copy[p]()
-        place_copy[p] = move(v["midz"].at[p], v["midy"].at[p], to_y, y_next == y)
+        place_copy[p] = move(part_of("midz", p), part_of("midy", p), to_y, y_here, y_away)
 
     def place_x(p):
         place_copy[p]()
-        place_copy[p] = move(v["midy"].at[p], cols_out.at[p], to_x, x_next == x)
+        place_copy[p] = move(part_of("midy", p), lambda: cols_out.at[p], to_x, x_here, x_away)
 
     def gram(p, k, right):
         value = dot3((v["oh"][k], v["ol"][k]), right)
@@ -330,7 +410,7 @@
         g = v[f"g{p}"].at[core]
         g[...] += v[f"gs{p}"][...]
         for s in range(1, 4):
-            a_copy[p, s] = send(g.at[(a_me + s) % 4], v[f"ga{p}"].at[s - 1], a_peer[s])
+            a_copy[p, s] = send(part_of(f"g{p}", core, a_at[s]), part_of(f"ga{p}", s - 1), a_peer[s])
 
     def reduce_b(p):
         g = v[f"g{p}"].at[core, a_me]
@@ -338,7 +418,7 @@
             a_copy[p, s].wait_recv()
         g[...] += v[f"ga{p}"][0] + v[f"ga{p}"][1] + v[f"ga{p}"][2]
         for s in range(1, 4):
-            b_copy[p, s] = send(g.at[(b_me + s) % 4], v[f"gb{p}"].at[s - 1], b_peer[s])
+            b_copy[p, s] = send(part_of(f"g{p}", core, a_me, b_at[s]), part_of(f"gb{p}", s - 1), b_peer[s])
 
     def reduce_x(p):
         for s in range(1, 4):
@@ -346,29 +426,29 @@
         gb, gx = v[f"gb{p}"], v[f"gx{p}"]
         gx[x] = v[f"g{p}"][core, a_me, b_me] + gb[0] + gb[1] + gb[2]
         for s in range(1, 4):
-            gx_copy[p, s] = send(gx.at[x], gx.at[x], x_peer[s])
+            gx_copy[p, s] = send(part_of(f"gx{p}", x), part_of(f"gx{p}", x), x_peer[s])
 
     def gather_b(p):
         for s in range(1, 4):
             gx_copy[p, s].wait_recv()
-        gx, res = v[f"gx{p}"], v[f"res{p}"].at[core, a_me, b_me]
-        res[...] = (gx[0] + gx[1]) + (gx[2] + gx[3])
-        for s in range(1, 4):
-            back[p, "b", s] = send(res, res, b_peer[s])
+        gx, res_at = v[f"gx{p}"], part_of(f"res{p}", core, a_me, b_me)
+        v[f"res{p}"][core, a_me, b_me] = (gx[0] + gx[1]) + (gx[2] + gx[3])
+        for s in range(1, 4):
+            back[p, "b", s] = send(res_at, res_at, b_peer[s])
 
     def gather_a(p):
         for s in range(1, 4):
             back[p, "b", s].wait_recv()
-        res = v[f"res{p}"].at[core, a_me]
-        for s in range(1, 4):
-            back[p, "a", s] = send(res, res, a_peer[s])
+        res_at = part_of(f"res{p}", core, a_me)
+        for s in range(1, 4):
+            back[p, "a", s] = send(res_at, res_at, a_peer[s])
 
     def gather_core(p):
         for key, copy in back.items():
             if key[:2] == (p, "a"):
                 copy.wait_recv()
-        res = v[f"res{p}"].at[core]
-        back[p, "core"] = send(res, res, sibling)
+        res_at = part_of(f"res{p}", core)
+        back[p, "core"] = send(res_at, res_at, sibling)
 
     def block(p, k):
         return v[f"res{p}"][:, :, :, k].reshape(W, W)
@@ -405,13 +485,26 @@
         pending.clear()
 
     steps = {
-        "prep": lambda p: prep(p, range(8)), "tile": tile, "handle": handle, "combine": combine,
-        "own": prep_own, "cross": prep_cross, "diag": start_diag, "final": final, "ra": reduce_a, "rb": reduce_b,
-        "rx": reduce_x, "gb": gather_b, "ga": gather_a, "gc": gather_core, "inv": diagonal, "pz": place_z,
-        "py": place_y, "px": place_x, "settle": settle,
+        "handle": handle, "combine": combine, "own": prep_own, "cross": prep_cross, "diag": start_diag,
+        "final": final, "ra": reduce_a, "rb": reduce_b, "rx": reduce_x, "gb": gather_b, "ga": gather_a,
+        "gc": gather_core, "inv": diagonal, "pz": place_z, "py": place_y, "px": place_x, "settle": settle,
     }
-    for name, *where in ORDER:
-        steps[name](*where)
+
+    def take(order):
+        for name, *where in order:
+            steps[name](*where)
+
+    @pl.loop(0, 16)
+    def _(step):
+        tile(step)
+        for i, order in enumerate(BETWEEN):
+            if order:
+                pl.when(step == i)(lambda order=order: take(order))
+
+    take(AFTER)
+    for p in range(PANELS):
+        for t in range(4):
+            sib_copy(p, t).wait_send()
     settle()
     for p in range(PANELS):
         place_copy[p]()
@@ -447,6 +540,8 @@
             pltpu.SemaphoreType.DMA((REMOTE,)),
             pltpu.SemaphoreType.DMA((REMOTE,)),
             pltpu.SemaphoreType.DMA((LOCAL,)),
+            pltpu.SemaphoreType.DMA((16,)),
+            pltpu.SemaphoreType.DMA((16,)),
         ],
         compiler_params=pltpu.CompilerParams(
             collective_id=0, has_side_effects=True, vmem_limit_bytes=VMEM_LIMIT

time: 83.9 us -> 77.4 us (0.923)
  Pallas kernels: 82.9 us -> 76.6 us
    pallas_call x1, Pallas kernels: 80.6 us -> 74.3 us  [shards(): pl.pallas_call(body, out_shape=tuple((pltpu.VMEM(shape, F32) for shape in...]
where the time goes in v4:
time: 77.4 us; the launch traced here: 77.2 us
  Pallas kernels  76.6 us (99%)
    pallas_call x1, Pallas kernels, shards(): pl.pallas_call(body, out_shape=tuple((pltpu.VMEM(shape, F32) for shape in...  74.3 us
    pallas_call x1, Pallas kernels, shards(): pl.pallas_call(copy_kernel, out_shape=tuple((jax.ShapeDtypeStruct(shape,...  2.22 us

profile of v4, /device:TPU:1, one launch (start us, length us, event | category | flops | bytes accessed | tf_op | source)
XLA Modules:
  0.0 77.2 jit_solution(14460202957391417569)
XLA Ops:
  0.6 74.3 %shard_map.68 = (f32[4,128,256]{2,1,0:T(8,128)S(1)}, f32[4,4,256,256]{3,2,1,0:T(8,128)S(1)}) custom-call(f32[2048,1024]{1,0:T(8,128)} %refs_0_.1, f32[4,2048,256]{2,1,0:T(8,128)} %refs_1_.1, f32[4,4,256,256]{3,2,1,0:T(8,128)} %refs_2_.1, f32[4,256,256]{2,1,0:T(8,128)} %refs_3_.1, s32[4,40]{1,0:T(4,128)} %refs_4_.1), custom_call_target="tpu_custom_call" | custom-call | flops 12884901888 | bytes 23068672 | tf_op jit(solution)/shard_map/pallas_call | solution.py:534
  75.0 2.2 %shard_map.69 = (f32[4,128,256]{2,1,0:T(8,128)}, f32[4,4,256,256]{3,2,1,0:T(8,128)}) custom-call(f32[4,128,256]{2,1,0:T(8,128)S(1)} %get-tuple-element.4.cols_in, f32[4,4,256,256]{3,2,1,0:T(8,128)S(1)} %get-tuple-element.5.inv_in), custom_call_target="tpu_custom_call" | custom-call | tf_op jit(solution)/shard_map/pallas_call | solution.py:553

commit v5 on v4

--- a/solution.py
+++ b/solution.py
@@ -81,43 +81,47 @@
     [
         ("handle", 3, 0),
     ],
-    [
-        ("handle", 3, 2),
-    ],
     [],
     [
-        ("handle", 3, 1), ("handle", 2, 0),
+        ("handle", 3, 3),
+    ],
+    [
+        ("handle", 3, 2), ("handle", 3, 1),
     ],
     [],
-    [],
-    [
-        ("combine", 3), ("handle", 2, 2), ("cross",), ("diag",), ("handle", 2, 1), ("handle", 1, 0),
-        ("own", 2),
-    ],
-    [
-        ("own", 1),
-    ],
-    [
-        ("combine", 2), ("own", 3), ("handle", 3, 3), ("own", 0), ("final", 3), ("pz", 3), ("handle", 1, 1),
-    ],
-    [
-        ("handle", 2, 3), ("handle", 1, 2), ("combine", 1), ("ra", 3),
-    ],
-    [
-        ("final", 2), ("pz", 2), ("handle", 0, 0), ("py", 3),
-    ],
-    [],
-    [
-        ("ra", 2), ("handle", 1, 3), ("handle", 0, 1), ("handle", 0, 2), ("rb", 3), ("combine", 0),
-        ("final", 1), ("pz", 1), ("py", 2),
+    [
+        ("handle", 2, 0),
+    ],
+    [
+        ("own", 3), ("combine", 3), ("cross",), ("diag",), ("handle", 1, 0), ("handle", 2, 3),
+    ],
+    [
+        ("handle", 2, 1), ("handle", 2, 2), ("own", 2), ("combine", 2), ("handle", 1, 1),
+    ],
+    [
+        ("own", 1), ("own", 0), ("final", 3), ("pz", 3),
+    ],
+    [
+        ("handle", 1, 2), ("combine", 1), ("ra", 3),
+    ],
+    [
+        ("final", 2), ("pz", 2), ("handle", 0, 0),
+    ],
+    [
+        ("ra", 2),
+    ],
+    [
+        ("rb", 3), ("handle", 0, 1), ("handle", 1, 3), ("py", 3), ("handle", 0, 2), ("combine", 0),
+        ("final", 1),
     ],
     [],
 ]
 AFTER = [
-    ("ra", 1), ("rb", 2), ("handle", 0, 3), ("rx", 3), ("final", 0), ("pz", 0), ("py", 1), ("px", 3),
-    ("ra", 0), ("rb", 1), ("rx", 2), ("gb", 3), ("py", 0), ("rx", 1), ("rb", 0), ("gb", 2), ("px", 2),
-    ("ga", 3), ("rx", 0), ("gb", 1), ("ga", 2), ("px", 0), ("gb", 0), ("gc", 3), ("ga", 1), ("ga", 0),
-    ("settle",), ("px", 1), ("inv", 3), ("gc", 2), ("gc", 1), ("inv", 2), ("gc", 0), ("inv", 1), ("inv", 0),
+    ("rb", 2), ("ra", 1), ("rx", 3), ("py", 2), ("pz", 1), ("handle", 0, 3), ("final", 0), ("rx", 2),
+    ("ra", 0), ("rb", 1), ("gb", 3), ("px", 3), ("pz", 0), ("py", 1), ("rb", 0), ("settle", 18), ("rx", 1), ("gb", 2),
+    ("px", 2), ("ga", 3), ("rx", 0), ("gb", 1), ("ga", 2), ("gb", 0), ("settle", 12), ("ga", 1), ("gc", 3), ("py", 0),
+    ("gc", 2), ("px", 1), ("inv", 3), ("ga", 0), ("settle", 6), ("ci", 2), ("inv", 2), ("gc", 1), ("ci", 1),
+    ("px", 0), ("inv", 1), ("gc", 0), ("ci", 0), ("inv", 0),
 ]
 LOCAL = 64
 
@@ -473,21 +477,19 @@
         inv_out[k, k] = value
         if k > 0:
             v["invt"][k] = value.T
-            cross_inverse(k - 1)
 
     def start_diag():
         diag_copy.wait()
         v["pre"][...] = v["diag"][3]
 
-    def settle():
-        for finish in pending:
-            finish()
-        pending.clear()
+    def settle(keep=0):
+        while len(pending) > keep:
+            pending.pop(0)()
 
     steps = {
         "handle": handle, "combine": combine, "own": prep_own, "cross": prep_cross, "diag": start_diag,
         "final": final, "ra": reduce_a, "rb": reduce_b, "rx": reduce_x, "gb": gather_b, "ga": gather_a,
-        "gc": gather_core, "inv": diagonal, "pz": place_z, "py": place_y, "px": place_x, "settle": settle,
+        "gc": gather_core, "inv": diagonal, "ci": cross_inverse, "pz": place_z, "py": place_y, "px": place_x, "settle": settle,
     }
 
     def take(order):

time: 77.4 us -> 75 us (0.969)
  Pallas kernels: 76.6 us -> 73.9 us
    pallas_call x1, Pallas kernels: 74.3 us -> 71.7 us  [shards(): pl.pallas_call(body, out_shape=tuple((pltpu.VMEM(shape, F32) for shape in...]
where the time goes in v5:
time: 75 us; the launch traced here: 74.6 us
  Pallas kernels  73.9 us (99%)
    pallas_call x1, Pallas kernels, shards(): pl.pallas_call(body, out_shape=tuple((pltpu.VMEM(shape, F32) for shape in...  71.7 us
    pallas_call x1, Pallas kernels, shards(): pl.pallas_call(copy_kernel, out_shape=tuple((jax.ShapeDtypeStruct(shape,...  2.22 us

profile of v5, /device:TPU:1, one launch (start us, length us, event | category | flops | bytes accessed | tf_op | source)
XLA Modules:
  0.0 74.6 jit_solution(1606997553628744682)
XLA Ops:
  0.6 71.7 %shard_map.68 = (f32[4,128,256]{2,1,0:T(8,128)S(1)}, f32[4,4,256,256]{3,2,1,0:T(8,128)S(1)}) custom-call(f32[2048,1024]{1,0:T(8,128)} %refs_0_.1, f32[4,2048,256]{2,1,0:T(8,128)} %refs_1_.1, f32[4,4,256,256]{3,2,1,0:T(8,128)} %refs_2_.1, f32[4,256,256]{2,1,0:T(8,128)} %refs_3_.1, s32[4,40]{1,0:T(4,128)} %refs_4_.1), custom_call_target="tpu_custom_call" | custom-call | flops 12884901888 | bytes 23068672 | tf_op jit(solution)/shard_map/pallas_call | solution.py:536
  72.3 2.2 %shard_map.69 = (f32[4,128,256]{2,1,0:T(8,128)}, f32[4,4,256,256]{3,2,1,0:T(8,128)}) custom-call(f32[4,128,256]{2,1,0:T(8,128)S(1)} %get-tuple-element.4.cols_in, f32[4,4,256,256]{3,2,1,0:T(8,128)S(1)} %get-tuple-element.5.inv_in), custom_call_target="tpu_custom_call" | custom-call | tf_op jit(solution)/shard_map/pallas_call | solution.py:555

commit v6 on v5

--- a/solution.py
+++ b/solution.py
@@ -118,10 +118,10 @@
 ]
 AFTER = [
     ("rb", 2), ("ra", 1), ("rx", 3), ("py", 2), ("pz", 1), ("handle", 0, 3), ("final", 0), ("rx", 2),
-    ("ra", 0), ("rb", 1), ("gb", 3), ("px", 3), ("pz", 0), ("py", 1), ("rb", 0), ("settle", 18), ("rx", 1), ("gb", 2),
-    ("px", 2), ("ga", 3), ("rx", 0), ("gb", 1), ("ga", 2), ("gb", 0), ("settle", 12), ("ga", 1), ("gc", 3), ("py", 0),
-    ("gc", 2), ("px", 1), ("inv", 3), ("ga", 0), ("settle", 6), ("ci", 2), ("inv", 2), ("gc", 1), ("ci", 1),
-    ("px", 0), ("inv", 1), ("gc", 0), ("ci", 0), ("inv", 0),
+    ("ra", 0), ("rb", 1), ("gb", 3), ("px", 3), ("pz", 0), ("py", 1), ("rb", 0), ("settle", 18), ("rx", 1),
+    ("gb", 2), ("px", 2), ("ga", 3), ("rx", 0), ("py", 0), ("gb", 1), ("ga", 2), ("gb", 0), ("settle", 12),
+    ("ga", 1), ("gc", 3), ("px", 1), ("gc", 2), ("px", 0), ("ga", 0), ("settle", 6), ("inv", 3), ("ci", 2),
+    ("inv", 2), ("gc", 1), ("ci", 1), ("inv", 1), ("gc", 0), ("ci", 0), ("inv", 0),
 ]
 LOCAL = 64
 

time: 75 us -> 74.5 us (level)
  no operation moved by 1% of the time
where the time goes in v6:
time: 74.5 us; the launch traced here: 74.3 us
  Pallas kernels  73.7 us (99%)
    pallas_call x1, Pallas kernels, shards(): pl.pallas_call(body, out_shape=tuple((pltpu.VMEM(shape, F32) for shape in...  71.5 us
    pallas_call x1, Pallas kernels, shards(): pl.pallas_call(copy_kernel, out_shape=tuple((jax.ShapeDtypeStruct(shape,...  2.22 us

profile of v6, /device:TPU:1, one launch (start us, length us, event | category | flops | bytes accessed | tf_op | source)
XLA Modules:
  0.0 74.3 jit_solution(8143392256871251051)
XLA Ops:
  0.6 71.5 %shard_map.68 = (f32[4,128,256]{2,1,0:T(8,128)S(1)}, f32[4,4,256,256]{3,2,1,0:T(8,128)S(1)}) custom-call(f32[2048,1024]{1,0:T(8,128)} %refs_0_.1, f32[4,2048,256]{2,1,0:T(8,128)} %refs_1_.1, f32[4,4,256,256]{3,2,1,0:T(8,128)} %refs_2_.1, f32[4,256,256]{2,1,0:T(8,128)} %refs_3_.1, s32[4,40]{1,0:T(4,128)} %refs_4_.1), custom_call_target="tpu_custom_call" | custom-call | flops 12884901888 | bytes 23068672 | tf_op jit(solution)/shard_map/pallas_call | solution.py:536
  72.1 2.2 %shard_map.69 = (f32[4,128,256]{2,1,0:T(8,128)}, f32[4,4,256,256]{3,2,1,0:T(8,128)}) custom-call(f32[4,128,256]{2,1,0:T(8,128)S(1)} %get-tuple-element.4.cols_in, f32[4,4,256,256]{3,2,1,0:T(8,128)S(1)} %get-tuple-element.5.inv_in), custom_call_target="tpu_custom_call" | custom-call | tf_op jit(solution)/shard_map/pallas_call | solution.py:555
